TPU v7x, 32 devices: a whole 2x2x4 slice. The times are simulated.
32 devices in a mesh: tm: 4 (over x, core), tile: 8 (over z, y).
Axes of the slice: x: 2, y: 2, z: 4, core: 2. Of those that a mesh axis runs over, the one named last changes fastest.
Arguments:
- basis: float32 [256, 128, 512], P(None, 'tile'), may hold values from -6 to 6
- diffusion: float32 [4, 128, 512], P('tm', 'tile'), may hold values from 0.12 to 0.24
- drift_x: float32 [4, 128, 512], P('tm', 'tile'), may hold values from -1 to 1
- drift_y: float32 [4, 128, 512], P('tm', 'tile'), may hold values from -1 to 1
- land_sea: int32 [128, 512], P('tile'), may hold values from 0 to 1, as said below
- obs_cells: int32 [4, 512], P('tm'), may hold values from 0 to 65535
- obs_values: float32 [4, 512], P('tm'), may hold values from -72 to 72
Outputs:
- group_coeffs: float32 [4, 2, 256], P('tm')
- end_fields: float32 [4, 128, 512], P('tm', 'tile')
Inputs may be any that keep to these rules, and one draw needn't show every extreme that they name: `land_sea`: only 0 and 1; both occur. `obs_cells`: cells may repeat within and across groups.
All inputs are finite; a program needn't handle non-finite values.
Results may differ from a plain program's by a relative error of at most 0.0003.
Values sent between devices are 32-bit elements; how exact they have to be, the bound alone decides.
A program may use at most 128 MiB of HBM per device.

v0:
```python
import jax
import jax.numpy as jnp
from jax import lax
from jax.sharding import PartitionSpec as P

STEPS = 6
NOBS = 512


q_inverse = 10.0
ridge = 0.1


def padded(cells, sides, width):
    for axis, dim in sides:
        count = lax.axis_size(axis)
        ends = count - 1
        head = lax.slice_in_dim(cells, 0, width, axis=dim)
        tail = lax.slice_in_dim(cells, cells.shape[dim] - width, cells.shape[dim], axis=dim)
        cells = jnp.concatenate(
            [
                lax.ppermute(tail, axis, [(i, (i + 1) % count) for i in range(ends)]),
                cells,
                lax.ppermute(head, axis, [((i + 1) % count, i) for i in range(ends)]),
            ],
            axis=dim,
        )
    return cells


def partner(block, axis, bit):
    count = lax.axis_size(axis)
    route = []
    for low in range(count):
        high = low | 1 << bit
        if high != low and high < count:
            route += [(low, high), (high, low)]
    return lax.ppermute(block, axis, route)


def precise_dot(first, second):
    return jnp.dot(first, second, precision=lax.Precision.HIGHEST)


def gain_fields(diffusion, drift_x, drift_y, sea_mask):
    return (
        1.0 - 4.0 * diffusion,
        diffusion * (1.0 - drift_x),
        diffusion * (1.0 + drift_x),
        diffusion * (1.0 - drift_y),
        diffusion * (1.0 + drift_y),
        sea_mask,
    )


def tangent_step(widened, gains):
    center_gain, east_gain, west_gain, north_gain, south_gain, sea_mask = gains
    center = widened[:, 1:-1]
    padded_y = jnp.pad(center, ((0, 0), (0, 0), (1, 1)))
    return sea_mask * (
        center_gain * center
        + east_gain * widened[:, 2:]
        + west_gain * widened[:, :-2]
        + north_gain * padded_y[:, :, 2:]
        + south_gain * padded_y[:, :, :-2]
    )


def chol_solve(factor, right):
    inner = lax.linalg.triangular_solve(factor, right, left_side=True, lower=True)
    return lax.linalg.triangular_solve(factor, inner, left_side=True, lower=True, transpose_a=True)


def merge_pair(left, right):
    left_upper, left_cross, left_lower, left_first, left_second = left
    right_upper, right_cross, right_lower, right_first, right_second = right
    width = left_upper.shape[0]
    factor = jnp.linalg.cholesky(left_lower + right_upper)
    both = chol_solve(factor, jnp.concatenate([left_cross.T, right_cross], axis=1))
    back_left = both[:, :width]
    back_right = both[:, width:]
    back_rhs = chol_solve(factor, (left_second + right_first)[:, None])[:, 0]
    merged = (
        left_upper - precise_dot(left_cross, back_left),
        -precise_dot(left_cross, back_right),
        right_lower - precise_dot(right_cross.T, back_right),
        left_first - precise_dot(left_cross, back_rhs),
        right_second - precise_dot(right_cross.T, back_rhs),
    )
    return (merged, (back_left, back_right, back_rhs))


def solve_root(block):
    upper, cross, lower, first, second = block
    width = upper.shape[0]
    system = jnp.concatenate(
        [jnp.concatenate([upper, cross], axis=1), jnp.concatenate([cross.T, lower], axis=1)], axis=0
    )
    factor = jnp.linalg.cholesky(system)
    answer = chol_solve(factor, jnp.concatenate([first, second])[:, None])[:, 0]
    return (answer[:width], answer[width:])


def shards(basis, diffusion, drift_x, drift_y, land_sea, obs_cells, obs_values):
    width = basis.shape[0]
    rows = basis.shape[1]
    columns = basis.shape[2]
    sea_mask = land_sea.astype(jnp.float32)
    gains = gain_fields(diffusion[0], drift_x[0], drift_y[0], sea_mask)
    field = basis
    for section in range(STEPS):
        widened = padded(field, (("tile", 1),), 1)
        field = tangent_step(widened, gains)
    flat_basis = basis.reshape(width, rows * columns)
    local_prop = precise_dot(flat_basis, field.reshape(width, rows * columns).T)
    offset = lax.axis_index("tile") * (rows * columns)
    local_cells = obs_cells[0] - offset
    inside = ((local_cells >= 0) & (local_cells < rows * columns)).astype(jnp.float32)
    obs_rows = (
        jnp.take(flat_basis, jnp.clip(local_cells, 0, rows * columns - 1), axis=1) * inside[None, :]
    )
    local_info = precise_dot(obs_rows, obs_rows.T)
    local_rhs = precise_dot(obs_rows, obs_values[0])
    prop_sum, info_sum, rhs_sum = lax.psum((local_prop, local_info, local_rhs), "tile")
    propagator = prop_sum / float(rows * columns * lax.axis_size("tile"))
    obs_info = info_sum / float(NOBS)
    obs_rhs = rhs_sum / float(NOBS)
    identity = jnp.eye(width, dtype=jnp.float32)
    block = (
        q_inverse * precise_dot(propagator.T, propagator) + ridge * identity,
        -q_inverse * propagator.T,
        (q_inverse + ridge) * identity + obs_info,
        jnp.zeros((width,), jnp.float32),
        obs_rhs,
    )
    group = lax.axis_index("tm")
    levels = lax.axis_size("tm").bit_length() - 1
    saved = []
    for level in range(levels):
        other = partner((block[0], block[1], block[2], block[3], block[4]), "tm", level)
        upper_half = group >> level & 1 == 1
        left = jax.tree.map(
            lambda first, second: jnp.where(upper_half, second, first), block, other
        )
        right = jax.tree.map(
            lambda first, second: jnp.where(upper_half, first, second), block, other
        )
        block, kept = merge_pair(left, right)
        saved.append(kept)
    start_state, end_state = solve_root(block)
    for level in reversed(range(levels)):
        back_left, back_right, back_rhs = saved[level]
        middle = back_rhs - precise_dot(back_left, start_state) - precise_dot(back_right, end_state)
        upper_half = group >> level & 1 == 1
        start_state = jnp.where(upper_half, middle, start_state)
        end_state = jnp.where(upper_half, end_state, middle)
    group_coeffs = jnp.stack([start_state, end_state])[None]
    end_fields = jnp.tensordot(end_state, basis, axes=1, precision=lax.Precision.HIGHEST)[None]
    return (group_coeffs, end_fields)


def solution(mesh):
    in_specs = (
        P(None, "tile", None),
        P("tm", "tile", None),
        P("tm", "tile", None),
        P("tm", "tile", None),
        P("tile", None),
        P("tm", None),
        P("tm", None),
    )
    out_specs = (P("tm", None, None), P("tm", "tile", None))
    return jax.shard_map(shards, mesh=mesh, in_specs=in_specs, out_specs=out_specs, check_vma=False)
```

profile of v0, /device:TPU:0, one launch (start us, length us, event | category | flops | bytes accessed | tf_op | source)
XLA Modules:
  0.0 727.5 jit_solution(1976326325573385900)
XLA Ops:
  25.7 9.9 %collective-permute-done.1 = f32[256,1,512]{2,0,1:T(8,128)S(1)} collective-permute-done((f32[256,1,512]{2,0,1:T(8,128)S(1)}, f32[256,1,512]{2,0,1:T(8,128)S(1)}, u32[]{:S(2)}, u32[]{:S(2)}) %collective-permute-start.1) | collective-permute-done | bytes 524320 | tf_op jit(solution)/shard_map/ppermute | solution.py:24
  35.6 11.4 %collective-permute-done.2 = f32[256,1,512]{2,0,1:T(8,128)S(1)} collective-permute-done((f32[256,1,512]{2,0,1:T(8,128)S(1)}, f32[256,1,512]{2,0,1:T(8,128)S(1)}, u32[]{:S(2)}, u32[]{:S(2)}) %collective-permute-start.2) | collective-permute-done | bytes 524320 | tf_op jit(solution)/shard_map/ppermute | solution.py:22
  47.0 19.7 %fusion.3 = f32[256,16,512]{2,0,1:T(8,128)} fusion(f32[256,16,512]{2,0,1:T(8,128)} %copy-done.1, f32[256,1,512]{2,0,1:T(8,128)S(1)} %collective-permute-done.2, f32[256,1,512]{2,0,1:T(8,128)S(1)} %collective-permute-done.1, f32[16,512]{1,0:T(8,128)S(1)} %get-tuple-element.149, f32[16,512]{1,0:T(8,128)S(1)} %get-tuple-element.150, ...), kind=kLoop, calls=%fused_computation.22 | loop fusion | flops 25165824 | bytes 18022400 | tf_op jit(solution)/shard_map/mul | solution.py:60
  74.3 10.1 %collective-permute-done.3 = f32[256,1,512]{2,0,1:T(8,128)S(1)} collective-permute-done((f32[256,1,512]{2,0,1:T(8,128)S(1)}, f32[256,1,512]{2,0,1:T(8,128)S(1)}, u32[]{:S(2)}, u32[]{:S(2)}) %collective-permute-start.3) | collective-permute-done | bytes 524320 | tf_op jit(solution)/shard_map/ppermute | solution.py:24
  84.4 11.4 %collective-permute-done.4 = f32[256,1,512]{2,0,1:T(8,128)S(1)} collective-permute-done((f32[256,1,512]{2,0,1:T(8,128)S(1)}, f32[256,1,512]{2,0,1:T(8,128)S(1)}, u32[]{:S(2)}, u32[]{:S(2)}) %collective-permute-start.4) | collective-permute-done | bytes 524320 | tf_op jit(solution)/shard_map/ppermute | solution.py:22
  95.8 19.7 %fusion.8 = f32[256,16,512]{2,0,1:T(8,128)} fusion(f32[256,16,512]{2,0,1:T(8,128)} %fusion.3, f32[256,1,512]{2,0,1:T(8,128)S(1)} %collective-permute-done.4, f32[256,1,512]{2,0,1:T(8,128)S(1)} %collective-permute-done.3, f32[16,512]{1,0:T(8,128)S(1)} %get-tuple-element.149, f32[16,512]{1,0:T(8,128)S(1)} %get-tuple-element.150, ...), kind=kLoop, calls=%fused_computation.27 | loop fusion | flops 25165824 | bytes 18022400 | tf_op jit(solution)/shard_map/mul | solution.py:60
  123.4 10.0 %collective-permute-done.5 = f32[256,1,512]{2,0,1:T(8,128)S(1)} collective-permute-done((f32[256,1,512]{2,0,1:T(8,128)S(1)}, f32[256,1,512]{2,0,1:T(8,128)S(1)}, u32[]{:S(2)}, u32[]{:S(2)}) %collective-permute-start.5) | collective-permute-done | bytes 524320 | tf_op jit(solution)/shard_map/ppermute | solution.py:24
  133.3 11.4 %collective-permute-done.6 = f32[256,1,512]{2,0,1:T(8,128)S(1)} collective-permute-done((f32[256,1,512]{2,0,1:T(8,128)S(1)}, f32[256,1,512]{2,0,1:T(8,128)S(1)}, u32[]{:S(2)}, u32[]{:S(2)}) %collective-permute-start.6) | collective-permute-done | bytes 524320 | tf_op jit(solution)/shard_map/ppermute | solution.py:22
  144.7 19.7 %fusion.13 = f32[256,16,512]{2,0,1:T(8,128)} fusion(f32[256,16,512]{2,0,1:T(8,128)} %fusion.8, f32[256,1,512]{2,0,1:T(8,128)S(1)} %collective-permute-done.6, f32[256,1,512]{2,0,1:T(8,128)S(1)} %collective-permute-done.5, f32[16,512]{1,0:T(8,128)S(1)} %get-tuple-element.149, f32[16,512]{1,0:T(8,128)S(1)} %get-tuple-element.150, ...), kind=kLoop, calls=%fused_computation.32 | loop fusion | flops 25165824 | bytes 18022400 | tf_op jit(solution)/shard_map/mul | solution.py:60
  172.0 10.1 %collective-permute-done.7 = f32[256,1,512]{2,0,1:T(8,128)S(1)} collective-permute-done((f32[256,1,512]{2,0,1:T(8,128)S(1)}, f32[256,1,512]{2,0,1:T(8,128)S(1)}, u32[]{:S(2)}, u32[]{:S(2)}) %collective-permute-start.7) | collective-permute-done | bytes 524320 | tf_op jit(solution)/shard_map/ppermute | solution.py:24
  182.2 11.4 %collective-permute-done.8 = f32[256,1,512]{2,0,1:T(8,128)S(1)} collective-permute-done((f32[256,1,512]{2,0,1:T(8,128)S(1)}, f32[256,1,512]{2,0,1:T(8,128)S(1)}, u32[]{:S(2)}, u32[]{:S(2)}) %collective-permute-start.8) | collective-permute-done | bytes 524320 | tf_op jit(solution)/shard_map/ppermute | solution.py:22
  193.5 19.7 %fusion.18 = f32[256,16,512]{2,0,1:T(8,128)} fusion(f32[256,16,512]{2,0,1:T(8,128)} %fusion.13, f32[256,1,512]{2,0,1:T(8,128)S(1)} %collective-permute-done.8, f32[256,1,512]{2,0,1:T(8,128)S(1)} %collective-permute-done.7, f32[16,512]{1,0:T(8,128)S(1)} %get-tuple-element.149, f32[16,512]{1,0:T(8,128)S(1)} %get-tuple-element.150, ...), kind=kLoop, calls=%fused_computation.37 | loop fusion | flops 25165824 | bytes 18022400 | tf_op jit(solution)/shard_map/mul | solution.py:60
  220.3 21.2 %collective-permute-done.10 = f32[256,1,512]{2,0,1:T(8,128)S(1)} collective-permute-done((f32[256,1,512]{2,0,1:T(8,128)S(1)}, f32[256,1,512]{2,0,1:T(8,128)S(1)}, u32[]{:S(2)}, u32[]{:S(2)}) %collective-permute-start.10) | collective-permute-done | bytes 524320 | tf_op jit(solution)/shard_map/ppermute | solution.py:22
  241.5 19.7 %fusion.23 = f32[256,16,512]{2,0,1:T(8,128)} fusion(f32[256,16,512]{2,0,1:T(8,128)} %fusion.18, f32[256,1,512]{2,0,1:T(8,128)S(1)} %collective-permute-done.10, f32[256,1,512]{2,0,1:T(8,128)S(1)} %collective-permute-done.9, f32[16,512]{1,0:T(8,128)S(1)} %get-tuple-element.149, f32[16,512]{1,0:T(8,128)S(1)} %get-tuple-element.150, ...), kind=kLoop, calls=%fused_computation.42 | loop fusion | flops 25165824 | bytes 18022400 | tf_op jit(solution)/shard_map/mul | solution.py:60
  268.9 9.9 %copy.45 = f32[256,16,512]{0,2,1:T(8,128)} copy(f32[256,16,512]{2,1,0:T(8,128)} %param.18) | data formatting | bytes 16777216 | tf_op args[0]
  289.5 43.2 %fusion.69 = f32[256,256]{0,1:T(8,128)} fusion(f32[256,16,512]{2,0,1:T(8,128)} %fusion.23, f32[256,1,512]{2,0,1:T(8,128)S(1)} %collective-permute-done.12, f32[256,1,512]{2,0,1:T(8,128)S(1)} %collective-permute-done.11, f32[16,512]{1,0:T(8,128)S(1)} %get-tuple-element.149, f32[16,512]{1,0:T(8,128)S(1)} %get-tuple-element.150, ...), kind=kOutput, calls=%fused_computation.102 | convolution fusion | flops 6467616768 | bytes 18284544 | tf_op jit(solution)/shard_map/dot_general | solution.py:42
  333.2 20.0 %psum.23 = f32[256]{0:T(256)S(1)} all-reduce(f32[256]{0:T(256)S(1)} %bitcast.400), channel_id=1, replica_groups=mesh['tm'=4,'tile'=8] {'tile'}, use_global_device_ids=true, to_apply=%region_6.9 | all-reduce | flops 256 | bytes 2048 | tf_op jit(solution)/shard_map/psum | solution.py:124
  353.8 52.9 %all-reduce.11.cloned.1.call-done = (f32[256,256]{0,1:T(8,128)}, f32[256,256]{0,1:T(8,128)}) async-done(((f32[256,256]{0,1:T(8,128)}, f32[256,256]{0,1:T(8,128)}), (f32[256,256]{0,1:T(8,128)}, f32[256,256]{0,1:T(8,128)})) %all-reduce.11.cloned.1.call-update) | async-done | bytes 524304 | tf_op jit(solution)/shard_map/psum | solution.py:124
  412.3 11.7 %cholesky.357 = f32[128,128]{1,0:T(8,128)S(1)} custom-call(f32[128,128]{1,0:T(8,128)S(1)} %cholesky.407), custom_call_target="Cholesky" | custom-call | tf_op jit(solution)/shard_map/jit(cholesky)/cholesky | solution.py:78
  434.4 11.7 %cholesky.367 = f32[128,128]{1,0:T(8,128)S(1)} custom-call(f32[128,128]{1,0:T(8,128)S(1)} %convolution_subtract_fusion.5), custom_call_target="Cholesky" | custom-call | tf_op jit(solution)/shard_map/jit(cholesky)/cholesky | solution.py:78
  452.7 20.1 %custom-call.59 = f32[2,128,128]{1,2,0:T(8,128)S(1)} custom-call(f32[2,128,128]{2,1,0:T(8,128)S(1)} %get-tuple-element.73), custom_call_target="InvertDiagBlocksLowerTriangular" | custom-call | tf_op jit(solution)/shard_map/triangular_solve/custom-call.10 | solution.py:71
  495.8 11.7 %cholesky.384 = f32[128,128]{1,0:T(8,128)S(1)} custom-call(f32[128,128]{1,0:T(8,128)S(1)} %cholesky.410), custom_call_target="Cholesky" | custom-call | tf_op jit(solution)/shard_map/jit(cholesky)/cholesky | solution.py:78
  517.8 11.9 %cholesky.394 = f32[128,128]{1,0:T(8,128)S(1)} custom-call(f32[128,128]{1,0:T(8,128)S(1)} %convolution_subtract_fusion.4), custom_call_target="Cholesky" | custom-call | tf_op jit(solution)/shard_map/jit(cholesky)/cholesky | solution.py:78
  536.5 19.7 %custom-call.64 = f32[2,128,128]{1,2,0:T(8,128)S(1)} custom-call(f32[2,128,128]{2,1,0:T(8,128)S(1)} %get-tuple-element.77), custom_call_target="InvertDiagBlocksLowerTriangular" | custom-call | tf_op jit(solution)/shard_map/triangular_solve/custom-call.10 | solution.py:71
  566.5 11.7 %cholesky.167 = f32[128,128]{1,0:T(8,128)S(1)} custom-call(f32[128,128]{1,0:T(8,128)S(1)} %cholesky.413), custom_call_target="Cholesky" | custom-call | tf_op jit(solution)/shard_map/jit(cholesky)/cholesky | solution.py:99
  589.5 12.1 %cholesky.190 = f32[128,128]{1,0:T(8,128)S(1)} custom-call(f32[128,128]{1,0:T(8,128)S(1)} %cholesky.417), custom_call_target="Cholesky" | custom-call | tf_op jit(solution)/shard_map/jit(cholesky)/cholesky | solution.py:99
  614.3 11.7 %cholesky.294 = f32[128,128]{1,0:T(8,128)S(1)} custom-call(f32[128,128]{1,0:T(8,128)S(1)} %cholesky.422), custom_call_target="Cholesky" | custom-call | tf_op jit(solution)/shard_map/jit(cholesky)/cholesky | solution.py:99
  626.7 9.9 %custom-call.67 = f32[1,128,128]{1,2,0:T(8,128)S(1)} custom-call(f32[1,128,128]{2,1,0:T(8,128)S(1)} %get-tuple-element.129), custom_call_target="InvertDiagBlocksLowerTriangular" | custom-call | tf_op jit(solution)/shard_map/jit(cholesky)/cholesky/custom-call.1 | solution.py:99
  637.3 11.7 %cholesky.307 = f32[128,128]{1,0:T(8,128)S(1)} custom-call(f32[128,128]{1,0:T(8,128)S(1)} %convolution_subtract_fusion.6), custom_call_target="Cholesky" | custom-call | tf_op jit(solution)/shard_map/jit(cholesky)/cholesky | solution.py:99
  652.4 10.4 %while.17 = (s32[]{:T(128)}, f32[512,512]{1,0:T(8,128)S(1)}, s32[4,2]{0,1:T(2,128)S(1)}, f32[4,128,128]{2,1,0:T(8,128)}, s32[]{:T(128)}) while((s32[]{:T(128)}, f32[512,512]{1,0:T(8,128)S(1)}, s32[4,2]{0,1:T(2,128)S(1)}, f32[4,128,128]{2,1,0:T(8,128)}, s32[]{:T(128)}) %tuple.113), condition=%wide.while_cond.4, body=%wide.while_body.4.sunk | while | flops 2 | bytes 132705 | solution.py:71
  662.8 40.3 %custom-call.48 = f32[4,128,128]{1,2,0:T(8,128)S(1)} custom-call(f32[4,128,128]{2,1,0:T(8,128)} %get-tuple-element.47), custom_call_target="InvertDiagBlocksLowerTriangular" | custom-call | tf_op jit(solution)/shard_map/triangular_solve | solution.py:71
  707.5 11.7 %fusion.228 = f32[1,16,512]{2,0,1:T(1,128)S(1)} fusion(f32[256,1,1]{0,1,2:T(1,128)S(1)} %bitcast.388, f32[256,16,512]{2,1,0:T(8,128)} %param.18), kind=kOutput, calls=%fused_computation.379 | convolution fusion | flops 25165824 | bytes 8422400 | tf_op jit(solution)/shard_map/dot_general | solution.py:158
  (239 shorter events, 187.8 us)
Async XLA Ops:
  7.2 325.6 %copy-start = (f32[1,512]{1,0:T(1,128)S(1)}, f32[1,512]{1,0:T(1,128)}, u32[]{:S(2)}) copy-start(f32[1,512]{1,0:T(1,128)} %param.24) | copy-start | bytes 6148
  7.2 18.5 %copy-start.7 = (s32[16,512]{1,0:T(8,128)S(1)}, s32[16,512]{1,0:T(8,128)}, u32[]{:S(2)}) copy-start(s32[16,512]{1,0:T(8,128)} %param.22) | copy-start | bytes 98308
  7.2 18.5 %copy-start.8 = (f32[1,16,512]{2,1,0:T(8,128)S(1)}, f32[1,16,512]{2,1,0:T(8,128)}, u32[]{:S(2)}) copy-start(f32[1,16,512]{2,1,0:T(8,128)} %param.19) | copy-start | bytes 98308
  7.2 18.5 %copy-start.9 = (f32[1,16,512]{2,1,0:T(8,128)S(1)}, f32[1,16,512]{2,1,0:T(8,128)}, u32[]{:S(2)}) copy-start(f32[1,16,512]{2,1,0:T(8,128)} %param.20) | copy-start | bytes 98308
  7.2 18.5 %copy-start.10 = (f32[1,16,512]{2,1,0:T(8,128)S(1)}, f32[1,16,512]{2,1,0:T(8,128)}, u32[]{:S(2)}) copy-start(f32[1,16,512]{2,1,0:T(8,128)} %param.21) | copy-start | bytes 98308
  7.2 399.5 %all-reduce.11.cloned.1.call-start = ((), (), s32[]{:S(2)}) async-start(), calls=%async_computation | async-start | bytes 1048576 | tf_op jit(solution)/shard_map/psum | solution.py:124
  15.5 3.2 copy-start.1
  18.8 16.8 %collective-permute-start.1 = (f32[256,1,512]{2,0,1:T(8,128)S(1)}, f32[256,1,512]{2,0,1:T(8,128)S(1)}, u32[]{:S(2)}, u32[]{:S(2)}) collective-permute-start(f32[256,1,512]{2,0,1:T(8,128)S(1)} %get-tuple-element.124), channel_id=1, source_target_pairs={{1,0},{2,1},{3,2},{4,3},{5,4},{6,5},{7,6},{9,8},{10,9},{11,10},{12... | collective-permute-start | bytes 1572872 | tf_op jit(solution)/shard_map/ppermute | solution.py:24
  20.1 26.9 %collective-permute-start.2 = (f32[256,1,512]{2,0,1:T(8,128)S(1)}, f32[256,1,512]{2,0,1:T(8,128)S(1)}, u32[]{:S(2)}, u32[]{:S(2)}) collective-permute-start(f32[256,1,512]{2,0,1:T(8,128)S(1)} %get-tuple-element.125), channel_id=1, source_target_pairs={{0,1},{1,2},{2,3},{3,4},{4,5},{5,6},{6,7},{8,9},{9,10},{10,11},{11... | collective-permute-start | bytes 1572872 | tf_op jit(solution)/shard_map/ppermute | solution.py:22
  67.9 16.5 %collective-permute-start.3 = (f32[256,1,512]{2,0,1:T(8,128)S(1)}, f32[256,1,512]{2,0,1:T(8,128)S(1)}, u32[]{:S(2)}, u32[]{:S(2)}) collective-permute-start(f32[256,1,512]{2,0,1:T(8,128)S(1)} %get-tuple-element.122), channel_id=1, source_target_pairs={{1,0},{2,1},{3,2},{4,3},{5,4},{6,5},{7,6},{9,8},{10,9},{11,10},{12... | collective-permute-start | bytes 1572872 | tf_op jit(solution)/shard_map/ppermute | solution.py:24
  69.2 26.6 %collective-permute-start.4 = (f32[256,1,512]{2,0,1:T(8,128)S(1)}, f32[256,1,512]{2,0,1:T(8,128)S(1)}, u32[]{:S(2)}, u32[]{:S(2)}) collective-permute-start(f32[256,1,512]{2,0,1:T(8,128)S(1)} %get-tuple-element.123), channel_id=1, source_target_pairs={{0,1},{1,2},{2,3},{3,4},{4,5},{5,6},{6,7},{8,9},{9,10},{10,11},{11... | collective-permute-start | bytes 1572872 | tf_op jit(solution)/shard_map/ppermute | solution.py:22
  116.8 16.5 %collective-permute-start.5 = (f32[256,1,512]{2,0,1:T(8,128)S(1)}, f32[256,1,512]{2,0,1:T(8,128)S(1)}, u32[]{:S(2)}, u32[]{:S(2)}) collective-permute-start(f32[256,1,512]{2,0,1:T(8,128)S(1)} %get-tuple-element.120), channel_id=1, source_target_pairs={{1,0},{2,1},{3,2},{4,3},{5,4},{6,5},{7,6},{9,8},{10,9},{11,10},{12... | collective-permute-start | bytes 1572872 | tf_op jit(solution)/shard_map/ppermute | solution.py:24
  118.1 26.6 %collective-permute-start.6 = (f32[256,1,512]{2,0,1:T(8,128)S(1)}, f32[256,1,512]{2,0,1:T(8,128)S(1)}, u32[]{:S(2)}, u32[]{:S(2)}) collective-permute-start(f32[256,1,512]{2,0,1:T(8,128)S(1)} %get-tuple-element.121), channel_id=1, source_target_pairs={{0,1},{1,2},{2,3},{3,4},{4,5},{5,6},{6,7},{8,9},{9,10},{10,11},{11... | collective-permute-start | bytes 1572872 | tf_op jit(solution)/shard_map/ppermute | solution.py:22
  165.7 16.5 %collective-permute-start.7 = (f32[256,1,512]{2,0,1:T(8,128)S(1)}, f32[256,1,512]{2,0,1:T(8,128)S(1)}, u32[]{:S(2)}, u32[]{:S(2)}) collective-permute-start(f32[256,1,512]{2,0,1:T(8,128)S(1)} %get-tuple-element.118), channel_id=1, source_target_pairs={{1,0},{2,1},{3,2},{4,3},{5,4},{6,5},{7,6},{9,8},{10,9},{11,10},{12... | collective-permute-start | bytes 1572872 | tf_op jit(solution)/shard_map/ppermute | solution.py:24
  167.0 53.3 %copy-start.11 = (s32[1,512]{1,0:T(1,128)S(1)}, s32[1,512]{1,0:T(1,128)}, u32[]{:S(2)}) copy-start(s32[1,512]{1,0:T(1,128)} %param.23) | copy-start | bytes 6148
  167.0 26.6 %collective-permute-start.8 = (f32[256,1,512]{2,0,1:T(8,128)S(1)}, f32[256,1,512]{2,0,1:T(8,128)S(1)}, u32[]{:S(2)}, u32[]{:S(2)}) collective-permute-start(f32[256,1,512]{2,0,1:T(8,128)S(1)} %get-tuple-element.119), channel_id=1, source_target_pairs={{0,1},{1,2},{2,3},{3,4},{4,5},{5,6},{6,7},{8,9},{9,10},{10,11},{11... | collective-permute-start | bytes 1572872 | tf_op jit(solution)/shard_map/ppermute | solution.py:22
  214.5 27.0 %collective-permute-start.10 = (f32[256,1,512]{2,0,1:T(8,128)S(1)}, f32[256,1,512]{2,0,1:T(8,128)S(1)}, u32[]{:S(2)}, u32[]{:S(2)}) collective-permute-start(f32[256,1,512]{2,0,1:T(8,128)S(1)} %get-tuple-element.117), channel_id=1, source_target_pairs={{0,1},{1,2},{2,3},{3,4},{4,5},{5,6},{6,7},{8,9},{9,10},{10,11},{11... | collective-permute-start | bytes 1572872 | tf_op jit(solution)/shard_map/ppermute | solution.py:22
  219.0 22.6 %collective-permute-start.9 = (f32[256,1,512]{2,0,1:T(8,128)S(1)}, f32[256,1,512]{2,0,1:T(8,128)S(1)}, u32[]{:S(2)}, u32[]{:S(2)}) collective-permute-start(f32[256,1,512]{2,0,1:T(8,128)S(1)} %get-tuple-element.116), channel_id=1, source_target_pairs={{1,0},{2,1},{3,2},{4,3},{5,4},{6,5},{7,6},{9,8},{10,9},{11,10},{12... | collective-permute-start | bytes 1572872 | tf_op jit(solution)/shard_map/ppermute | solution.py:24
  262.5 23.3 %collective-permute-start.11 = (f32[256,1,512]{2,0,1:T(8,128)S(1)}, f32[256,1,512]{2,0,1:T(8,128)S(1)}, u32[]{:S(2)}, u32[]{:S(2)}) collective-permute-start(f32[256,1,512]{2,0,1:T(8,128)S(1)} %get-tuple-element.114), channel_id=1, source_target_pairs={{1,0},{2,1},{3,2},{4,3},{5,4},{6,5},{7,6},{9,8},{10,9},{11,10},{12... | collective-permute-start | bytes 1572872 | tf_op jit(solution)/shard_map/ppermute | solution.py:24
  263.8 25.7 %collective-permute-start.12 = (f32[256,1,512]{2,0,1:T(8,128)S(1)}, f32[256,1,512]{2,0,1:T(8,128)S(1)}, u32[]{:S(2)}, u32[]{:S(2)}) collective-permute-start(f32[256,1,512]{2,0,1:T(8,128)S(1)} %get-tuple-element.115), channel_id=1, source_target_pairs={{0,1},{1,2},{2,3},{3,4},{4,5},{5,6},{6,7},{8,9},{9,10},{10,11},{11... | collective-permute-start | bytes 1572872 | tf_op jit(solution)/shard_map/ppermute | solution.py:22
  353.2 56.6 %collective-permute-start.14 = (f32[256]{0:T(256)S(1)}, f32[256]{0:T(256)S(1)}, u32[]{:S(2)}, u32[]{:S(2)}) collective-permute-start(f32[256]{0:T(256)S(1)} %broadcast_multiply_fusion), channel_id=1, source_target_pairs={{0,8},{8,0},{16,24},{24,16},{1,9},{9,1},{17,25},{25,17},{2,10},{10... | collective-permute-start | bytes 3080 | tf_op jit(solution)/shard_map/ppermute | solution.py:38
  353.3 56.5 %collective-permute-start.15 = (f32[256]{0:T(256)S(1)}, f32[256]{0:T(256)S(1)}, u32[]{:S(2)}, u32[]{:S(2)}) collective-permute-start(f32[256]{0:T(256)S(1)} %broadcast_in_dim.20), channel_id=1, source_target_pairs={{0,8},{8,0},{16,24},{24,16},{1,9},{9,1},{17,25},{25,17},{2,10},{10... | collective-permute-start | bytes 3080 | tf_op jit(solution)/shard_map/ppermute | solution.py:38
  406.7 69.3 %copy-start.4 = (f32[256,256]{0,1:T(8,128)S(1)}, f32[256,256]{0,1:T(8,128)}, u32[]{:S(2)}) copy-start(f32[256,256]{0,1:T(8,128)} %get-tuple-element.105) | copy-start | bytes 786436
  407.7 3.3 collective-permute-start
  409.2 72.9 %copy-start.3 = (f32[256,256]{0,1:T(8,128)S(1)}, f32[256,256]{0,1:T(8,128)}, u32[]{:S(2)}) copy-start(f32[256,256]{0,1:T(8,128)} %get-tuple-element.104) | copy-start | bytes 786436
  409.3 1.8 collective-permute-start.13
  410.8 63.1 %collective-permute-start.16 = (f32[256,256]{1,0:T(8,128)S(1)}, f32[256,256]{1,0:T(8,128)S(1)}, u32[]{:S(2)}, u32[]{:S(2)}) collective-permute-start(f32[256,256]{1,0:T(8,128)S(1)} %multiply_bitcast_fusion), channel_id=1, source_target_pairs={{0,8},{8,0},{16,24},{24,16},{1,9},{9,1},{17,25},{25,17},{2,10},{10... | collective-permute-start | bytes 786440 | tf_op jit(solution)/shard_map/ppermute | solution.py:38
  474.5 11.2 %collective-permute-start.19 = (f32[256]{0:T(256)S(1)}, f32[256]{0:T(256)S(1)}, u32[]{:S(2)}, u32[]{:S(2)}) collective-permute-start(f32[256]{0:T(256)S(1)} %select_subtract_fusion.7), channel_id=1, source_target_pairs={{0,16},{16,0},{8,24},{24,8},{1,17},{17,1},{9,25},{25,9},{2,18},{18... | collective-permute-start | bytes 3080 | tf_op jit(solution)/shard_map/ppermute | solution.py:38
  476.4 9.3 %collective-permute-start.20 = (f32[256]{0:T(256)S(1)}, f32[256]{0:T(256)S(1)}, u32[]{:S(2)}, u32[]{:S(2)}) collective-permute-start(f32[256]{0:T(256)S(1)} %select_subtract_fusion.6), channel_id=1, source_target_pairs={{0,16},{16,0},{8,24},{24,8},{1,17},{17,1},{9,25},{25,9},{2,18},{18... | collective-permute-start | bytes 3080 | tf_op jit(solution)/shard_map/ppermute | solution.py:38
  480.6 9.2 %collective-permute-start.18 = (f32[256,256]{0,1:T(8,128)S(1)}, f32[256,256]{0,1:T(8,128)S(1)}, u32[]{:S(2)}, u32[]{:S(2)}) collective-permute-start(f32[256,256]{0,1:T(8,128)S(1)} %select_subtract_fusion.2), channel_id=1, source_target_pairs={{0,16},{16,0},{8,24},{24,8},{1,17},{17,1},{9,25},{25,9},{2,18},{18... | collective-permute-start | bytes 786440 | tf_op jit(solution)/shard_map/ppermute | solution.py:38
  482.8 12.7 %collective-permute-start.17 = (f32[256,256]{0,1:T(8,128)S(1)}, f32[256,256]{0,1:T(8,128)S(1)}, u32[]{:S(2)}, u32[]{:S(2)}) collective-permute-start(f32[256,256]{0,1:T(8,128)S(1)} %select_subtract_fusion.3), channel_id=1, source_target_pairs={{0,16},{16,0},{8,24},{24,8},{1,17},{17,1},{9,25},{25,9},{2,18},{18... | collective-permute-start | bytes 786440 | tf_op jit(solution)/shard_map/ppermute | solution.py:38
  483.4 73.9 %collective-permute-start.21 = (f32[256,256]{1,0:T(8,128)S(1)}, f32[256,256]{1,0:T(8,128)S(1)}, u32[]{:S(2)}, u32[]{:S(2)}) collective-permute-start(f32[256,256]{1,0:T(8,128)S(1)} %convolution_negate_fusion.1), channel_id=1, source_target_pairs={{0,16},{16,0},{8,24},{24,8},{1,17},{17,1},{9,25},{25,9},{2,18},{18... | collective-permute-start | bytes 786440 | tf_op jit(solution)/shard_map/ppermute | solution.py:38
  (3 other events, 3.5 us)
Sparse Core Ops, SparseCore 0:
  332.8 73.7 all-reduce.10
where the time goes:
time: 737 us; the launch traced here: 728 us
  other arithmetic  334 us (45%)
  waiting for transfers between devices  173 us (23%)
  matrix products  78.6 us (11%)
  local copies, waits for them, and re-layouts  55.9 us (8%)
  starting transfers between devices  45.2 us (6%)
  between operations  20.6 us (3%)
  blocking collectives  20 us (3%)
    mul x5, other arithmetic, tangent_step(): sea_mask * (center_gain * center + east_gain * widened[:, 2:] + west_gain...  98.5 us
    another operation x12, other arithmetic, chol_solve(): lax.linalg.triangular_solve(factor, inner, left_side=True, lower=True, tr...  80.3 us
    another operation x15, other arithmetic, solve_root(): factor = jnp.linalg.cholesky(system)  79.6 us
    ppermute x6, waiting for transfers between devices, padded(): lax.ppermute(tail, axis, [(i, (i + 1) % count) for i in range(ends)])  70.5 us
    another operation x13, other arithmetic, merge_pair(): factor = jnp.linalg.cholesky(left_lower + right_upper)  68.8 us
    psum x1, waiting for transfers between devices, shards(): lax.psum((local_prop, local_info, local_rhs), 'tile')  52.9 us
    dot_general x18, matrix products, precise_dot(): return jnp.dot(first, second, precision=lax.Precision.HIGHEST)  52.7 us
    ppermute x6, waiting for transfers between devices, padded(): lax.ppermute(head, axis, [((i + 1) % count, i) for i in range(ends)])  40.1 us
  transfers between devices with their start and end apart: 23, of which 13 were waited for; matrix products, arithmetic and copies ran while one was open for 20% of the time, Pallas kernels for 0%

commit v1 on v0

v1 whole, which is shorter than its diff:
```python
import functools

import jax
import jax.numpy as jnp
from jax import lax
from jax.experimental import pallas as pl
from jax.experimental.pallas import tpu as pltpu
from jax.sharding import PartitionSpec as P

STEPS = 6
HALF = STEPS // 2

q_inverse = 10.0
ridge = 0.1

NT = (((1,), (1,)), ((), ()))
NN = (((1,), (0,)), ((), ()))
TN = (((0,), (0,)), ((), ()))


def split(x):
    high = x.astype(jnp.bfloat16)
    return high, (x - high.astype(jnp.float32)).astype(jnp.bfloat16)


def dot16(a, b, dims):
    return lax.dot_general(a, b, dims, preferred_element_type=jnp.float32)


def dot32(a, b, dims=NN):
    return lax.dot_general(
        a, b, dims, precision=lax.Precision.HIGHEST, preferred_element_type=jnp.float32
    )


def obs_kernel(rows, basis_ref, counts_ref, weights_ref, info_ref, rhs_ref):
    info_ref[...] = jnp.zeros_like(info_ref)
    rhs_ref[...] = jnp.zeros_like(rhs_ref)

    def row(r, _):
        x = basis_ref[r]
        y = x * counts_ref[pl.ds(r, 1), :]
        z = x * weights_ref[pl.ds(r, 1), :]
        xh, xl = split(x)
        yh, yl = split(y)
        info_ref[...] += dot16(xh, yh, NT) + dot16(xh, yl, NT) + dot16(xl, yh, NT)
        part = z[:, :128]
        for c in range(128, z.shape[1], 128):
            part += z[:, c : c + 128]
        rhs_ref[...] += part
        return 0

    lax.fori_loop(0, rows, row, 0)


def stencil_kernel(
    rows, block, basis_ref, halo_ref, fg_ref, lg_ref, prop_ref, gf, gl, f1, l1, f2, l2, fh, fl, lh, ll
):
    width, columns = basis_ref.shape[1:]
    halves = block // 8
    for which, (src, dst) in enumerate(((fg_ref, gf), (lg_ref, gl))):
        for i in range(5):
            for r in range(src.shape[1]):
                dst[i, r] = jnp.broadcast_to(src[i, r : r + 1, :], (8, columns))

    def rolled(x):
        return pltpu.roll(x, columns - 1, 1), pltpu.roll(x, 1, 1)

    def update(g, r, center, east, west, north, south):
        return (
            g[0, r] * center + g[1, r] * east + g[2, r] * west + g[3, r] * north + g[4, r] * south
        )

    def fields(kb, _):
        k = pl.multiple_of(kb * block, block)

        def load(r, h):
            if r < 0:
                return halo_ref[r + HALF, pl.ds(k + 8 * h, 8), :]
            if r >= rows:
                return halo_ref[r - rows + HALF, pl.ds(k + 8 * h, 8), :]
            return basis_ref[r, pl.ds(k + 8 * h, 8), :]

        edge = HALF - 1
        before = [load(-edge - 1, h) for h in range(halves)]
        here = [load(-edge, h) for h in range(halves)]
        for r in range(-edge, rows + edge):
            after = [load(r + 1, h) for h in range(halves)]
            for h in range(halves):
                north, south = rolled(here[h])
                f1[r + edge, h] = update(gf, r + edge, here[h], after[h], before[h], north, south)
                l1[r + edge, h] = update(gl, r + edge, here[h], after[h], before[h], north, south)
            before, here = here, after
        for g, s1, s2, high, low in ((gf, f1, f2, fh, fl), (gl, l1, l2, lh, ll)):
            src, dst = s1, s2
            for step in range(1, HALF):
                reach = HALF - 1 - step
                before = [src[edge - reach - 1, h] for h in range(halves)]
                here = [src[edge - reach, h] for h in range(halves)]
                for r in range(-reach, rows + reach):
                    after = [src[r + 1 + edge, h] for h in range(halves)]
                    new = []
                    for h in range(halves):
                        north, south = rolled(here[h])
                        new.append(update(g, r + edge, here[h], after[h], before[h], north, south))
                    if step < HALF - 1:
                        for h in range(halves):
                            dst[r + edge, h] = new[h]
                    else:
                        a, b = split(jnp.concatenate(new, axis=0))
                        high[r, pl.ds(k, block), :] = a
                        low[r, pl.ds(k, block), :] = b
                    before, here = here, after
                src, dst = dst, src
        return 0

    lax.fori_loop(0, width // block, fields, 0)
    prop_ref[...] = jnp.zeros_like(prop_ref)

    def row(r, _):
        prop_ref[...] += (
            dot16(lh[r], fh[r], NT) + dot16(lh[r], fl[r], NT) + dot16(ll[r], fh[r], NT)
        )
        return 0

    lax.fori_loop(0, rows, row, 0)


def eye_of(n):
    i = lax.broadcasted_iota(jnp.int32, (n, n), 0)
    j = lax.broadcasted_iota(jnp.int32, (n, n), 1)
    return (i == j).astype(jnp.float32)


def invert(mats, invs, tmps):
    n = mats[0].shape[0]
    eye = eye_of(n)
    size = 0.0
    for a, x, t in zip(mats, invs, tmps):
        scale = 1.0 / jnp.max(jnp.sum(jnp.abs(a[...]), axis=0, keepdims=True))
        r = eye - scale * a[...]
        t[...] = r
        x[...] = scale * (eye + r)
        size = jnp.maximum(size, jnp.sum(r * r))

    def grow(carry):
        it, _ = carry
        size = 0.0
        for x, t in zip(invs, tmps):
            r = dot32(t[...], t[...])
            t[...] = r
            x[...] += dot32(x[...], r)
            size = jnp.maximum(size, jnp.sum(r * r))
        return it + 1, size

    lax.while_loop(lambda c: (c[1] > 1e-4) & (c[0] < 30), grow, (0, size))

    def correct(carry):
        it, _ = carry
        size = 0.0
        for a, x in zip(mats, invs):
            r = eye - dot32(a[...], x[...])
            x[...] += dot32(x[...], r)
            size = jnp.maximum(size, jnp.sum(r * r))
        return it + 1, size

    lax.while_loop(lambda c: (c[1] > 1e-7) & (c[0] < 5), correct, (0, jnp.float32(1.0)))


def join_kernel(groups, scale_prop, scale_obs, prop_ref, info_ref, rhs_ref, out_ref, s, x, t, w):
    n = prop_ref.shape[1]
    middle = groups // 2
    q = q_inverse
    eye = eye_of(n)

    def prop(g):
        return prop_ref[g] * scale_prop

    def diagonal(i):
        value = ridge * eye
        if i < groups:
            p = prop(i)
            value = value + q * dot32(p, p, TN)
        if i > 0:
            value = value + (q * eye + info_ref[i - 1] * scale_obs)
            if i < groups:
                value = value + ridge * eye
        return value

    def right(i):
        if i == 0:
            return jnp.zeros((8, n), jnp.float32)
        return jnp.broadcast_to(rhs_ref[i - 1 : i, :] * scale_obs, (8, n))

    for i in range(groups + 1):
        s[i] = diagonal(i)
    vec = [right(i) for i in range(groups + 1)]
    for level in range(max(middle, groups - middle)):
        top = level if level < middle else None
        low = groups - level if groups - level > middle else None
        todo = [i for i in (top, low) if i is not None]
        invert([s.at[i] for i in todo], [x.at[i] for i in todo], [t.at[i] for i in todo])
        for i in todo:
            if i == top:
                p = prop(i)
                w[i] = q * dot32(x[i], p, NT)
                s[i + 1] -= q * dot32(p, w[i])
                vec[i + 1] = vec[i + 1] + dot32(vec[i], w[i])
            else:
                p = prop(i - 1)
                w[i] = q * dot32(x[i], p)
                s[i - 1] -= q * dot32(p, w[i], TN)
                vec[i - 1] = vec[i - 1] + dot32(vec[i], w[i])
    invert([s.at[middle]], [x.at[middle]], [t.at[middle]])
    state = {middle: dot32(vec[middle], x[middle])}
    for i in range(middle - 1, -1, -1):
        state[i] = dot32(vec[i], x[i]) + dot32(state[i + 1], w[i], NT)
    for i in range(middle + 1, groups + 1):
        state[i] = dot32(vec[i], x[i]) + dot32(state[i - 1], w[i], NT)
    for i in range(groups + 1):
        out_ref[i : i + 1, :] = state[i][:1]


VMEM = pltpu.VMEM


def shift(cells, width, dim):
    count = lax.axis_size("tile")
    head = lax.slice_in_dim(cells, 0, width, axis=dim)
    tail = lax.slice_in_dim(cells, cells.shape[dim] - width, cells.shape[dim], axis=dim)
    return (
        lax.ppermute(tail, "tile", [(i, i + 1) for i in range(count - 1)]),
        lax.ppermute(head, "tile", [(i + 1, i) for i in range(count - 1)]),
    )


def moved(x, by, dim):
    zero = jnp.zeros_like(lax.slice_in_dim(x, 0, 1, axis=dim))
    if by > 0:
        return jnp.concatenate([lax.slice_in_dim(x, 1, x.shape[dim], axis=dim), zero], axis=dim)
    return jnp.concatenate([zero, lax.slice_in_dim(x, 0, x.shape[dim] - 1, axis=dim)], axis=dim)


def shards(basis, diffusion, drift_x, drift_y, land_sea, obs_cells, obs_values):
    width, rows, columns = basis.shape
    nobs = obs_cells.shape[1]
    groups = lax.axis_size("tm")
    tiles = lax.axis_size("tile")
    group = lax.axis_index("tm")

    share = width // groups
    by_row = basis.transpose(1, 0, 2)
    mine = lax.dynamic_slice_in_dim(by_row, group * share, share, axis=1)
    above, below = shift(mine, HALF, 0)
    halo = lax.all_gather(jnp.concatenate([above, below], axis=0), "tm", axis=1, tiled=True)

    cells = jnp.stack(
        [diffusion[0], drift_x[0], drift_y[0], land_sea.astype(jnp.float32)], axis=0
    )
    before, after = shift(cells, HALF, 1)
    cells = jnp.concatenate([before, cells, after], axis=1)
    d, dx, dy, sea = cells[0], cells[1], cells[2], cells[3]
    column = lax.broadcasted_iota(jnp.int32, d.shape, 1)
    center = sea * (1.0 - 4.0 * d)
    east = sea * (d * (1.0 - dx))
    west = sea * (d * (1.0 + dx))
    north = jnp.where(column == columns - 1, 0.0, sea * (d * (1.0 - dy)))
    south = jnp.where(column == 0, 0.0, sea * (d * (1.0 + dy)))
    forward = jnp.stack([center, east, west, north, south])[:, 1:-1]
    backward = jnp.stack(
        [center, moved(west, 1, 0), moved(east, -1, 0), moved(south, 1, 1), moved(north, -1, 1)]
    )[:, 1:-1]

    offset = lax.axis_index("tile") * (rows * columns)
    local = obs_cells[0] - offset
    inside = (local >= 0) & (local < rows * columns)
    row_of = jnp.where(inside, local // columns, -1)
    col_of = local % columns
    in_row = lax.broadcasted_iota(jnp.int32, (rows, nobs), 0) == row_of[None, :]
    in_col = (lax.broadcasted_iota(jnp.int32, (columns, nobs), 0) == col_of[None, :]).astype(
        jnp.float32
    )
    hits = jnp.concatenate(
        [in_row.astype(jnp.float32), jnp.where(in_row, obs_values[0][None, :], 0.0)], axis=0
    )
    hits = dot32(hits, in_col, NT)

    info, rhs = pl.pallas_call(
        functools.partial(obs_kernel, rows),
        out_shape=(
            jax.ShapeDtypeStruct((width, width), jnp.float32),
            jax.ShapeDtypeStruct((width, 128), jnp.float32),
        ),
        in_specs=[pl.BlockSpec(memory_space=VMEM)] * 3,
        out_specs=[pl.BlockSpec(memory_space=VMEM)] * 2,
        compiler_params=pltpu.CompilerParams(vmem_limit_bytes=32 << 20),
        cost_estimate=pl.CostEstimate(
            flops=6 * width * width * rows * columns,
            bytes_accessed=4 * width * rows * columns,
            transcendentals=0,
        ),
        name="obs_info",
    )(by_row, hits[:rows], hits[rows:])

    block = 16
    edge_rows = rows + 2 * (HALF - 1)
    prop = pl.pallas_call(
        functools.partial(stencil_kernel, rows, block),
        out_shape=jax.ShapeDtypeStruct((width, width), jnp.float32),
        in_specs=[pl.BlockSpec(memory_space=VMEM)] * 4,
        out_specs=pl.BlockSpec(memory_space=VMEM),
        scratch_shapes=[VMEM((5, edge_rows, 8, columns), jnp.float32)] * 2
        + [VMEM((edge_rows, block // 8, 8, columns), jnp.float32)] * 4
        + [VMEM((rows, width, columns), jnp.bfloat16)] * 4,
        compiler_params=pltpu.CompilerParams(vmem_limit_bytes=48 << 20),
        cost_estimate=pl.CostEstimate(
            flops=66 * width * rows * columns,
            bytes_accessed=4 * width * rows * columns,
            transcendentals=0,
        ),
        name="propagate",
    )(by_row, halo, forward, backward)

    packed = jnp.concatenate([prop, info, jnp.sum(rhs, axis=1)[None, :]], axis=0)
    packed = lax.psum(packed, "tile")
    packed = lax.all_gather(packed, "tm", axis=0)
    states = pl.pallas_call(
        functools.partial(
            join_kernel, groups, 1.0 / (rows * columns * tiles), 1.0 / nobs
        ),
        out_shape=jax.ShapeDtypeStruct((groups + 1, width), jnp.float32),
        in_specs=[pl.BlockSpec(memory_space=VMEM)] * 3,
        out_specs=pl.BlockSpec(memory_space=VMEM),
        scratch_shapes=[VMEM((groups + 1, width, width), jnp.float32)] * 4,
        compiler_params=pltpu.CompilerParams(vmem_limit_bytes=48 << 20),
        name="join",
    )(packed[:, :width], packed[:, width : 2 * width], packed[:, 2 * width])
    coeffs = lax.dynamic_slice_in_dim(states, group, 2, axis=0)
    end_fields = jnp.sum(coeffs[1][:, None, None] * basis, axis=0)
    return coeffs[None], end_fields[None]


def solution(mesh):
    in_specs = (
        P(None, "tile", None),
        P("tm", "tile", None),
        P("tm", "tile", None),
        P("tm", "tile", None),
        P("tile", None),
        P("tm", None),
        P("tm", None),
    )
    out_specs = (P("tm", None, None), P("tm", "tile", None))
    return jax.shard_map(shards, mesh=mesh, in_specs=in_specs, out_specs=out_specs, check_vma=False)
```

time: 737 us -> 265 us (0.36); the launches traced: 728 us -> 265 us
  other arithmetic: 334 us -> 6.83 us
  Pallas kernels: 0 us -> 84.6 us
  matrix products: 78.6 us -> 0.59 us
  waiting for transfers between devices: 173 us -> 124 us
  local copies, waits for them, and re-layouts: 55.9 us -> 22.5 us
  starting transfers between devices: 45.2 us -> 12 us
  blocking collectives: 20 us -> 0 us
    another operation x40 -> x1, other arithmetic: 229 us -> 0.01 us  [shards(): jnp.stack([diffusion[0], drift_x[0], drift_y[0], land_sea.astype(jnp.floa...]
    ppermute x22 -> x4, waiting for transfers between devices: 120 us -> 15.5 us  [the longest x2 15.5 us: shift(): lax.ppermute(tail, 'tile', [(i, i + 1) for i in range(count - 1)])]
    mul x8 -> x1, other arithmetic: 99.5 us -> 0.02 us  [shards(): north = jnp.where(column == columns - 1, 0.0, sea * (d * (1.0 - dy)))]
    pallas_call x0 -> x3, Pallas kernels: none -> 84.6 us  [the longest x1 39.5 us: shards(): pl.pallas_call(functools.partial(join_kernel, groups, 1.0 / (rows * colum...]
    dot_general x19 -> x1, matrix products: 64.4 us -> 0.59 us  [dot32(): lax.dot_general(a, b, dims, precision=lax.Precision.HIGHEST, preferred_el...]
    all_gather x0 -> x2, waiting for transfers between devices: none -> 36.2 us  [the longest x1 23.6 us: shards(): packed = lax.all_gather(packed, 'tm', axis=0)]
    ppermute x22 -> x4, starting transfers between devices: 45.1 us -> 11.9 us  [the longest x2 9.28 us: shift(): lax.ppermute(tail, 'tile', [(i, i + 1) for i in range(count - 1)])]
    psum x1 -> x0, blocking collectives: 20 us -> none  [shards(): lax.psum((local_prop, local_info, local_rhs), 'tile')]
  transfers between devices with their start and end apart: 23 -> 7, of which waited for: 13 -> 4; matrix products, arithmetic and copies ran while one was open for 20% -> 0% of each run, Pallas kernels for 0% -> 3%
where the time goes in v1:
time: 265 us
  waiting for transfers between devices  124 us (47%)
  Pallas kernels  84.6 us (32%)
  local copies, waits for them, and re-layouts  22.5 us (8%)
  between operations  14.1 us (5%)
  starting transfers between devices  12 us (5%)
  other arithmetic  6.83 us (3%)
    psum x1, waiting for transfers between devices, shards(): packed = lax.psum(packed, 'tile')  72.5 us
    pallas_call x1, Pallas kernels, shards(): pl.pallas_call(functools.partial(join_kernel, groups, 1.0 / (rows * colum...  39.5 us
    pallas_call x1, Pallas kernels, shards(): pl.pallas_call(functools.partial(stencil_kernel, rows, block), out_shape=...  38 us
    all_gather x1, waiting for transfers between devices, shards(): packed = lax.all_gather(packed, 'tm', axis=0)  23.6 us
    unnamed x22, local copies, waits for them, and re-layouts  17.3 us
    ppermute x2, waiting for transfers between devices, shift(): lax.ppermute(tail, 'tile', [(i, i + 1) for i in range(count - 1)])  15.5 us
    all_gather x1, waiting for transfers between devices, shards(): lax.all_gather(jnp.concatenate([above, below], axis=0), 'tm', axis=1, til...  12.5 us
    ppermute x2, starting transfers between devices, shift(): lax.ppermute(tail, 'tile', [(i, i + 1) for i in range(count - 1)])  9.28 us
  transfers between devices with their start and end apart: 7, of which 4 were waited for; matrix products, arithmetic and copies ran while one was open for 0% of the time, Pallas kernels for 3%

profile of v1, /device:TPU:0, one launch (start us, length us, event | category | flops | bytes accessed | tf_op | source)
XLA Modules:
  0.0 264.8 jit_solution(3572921925295152531)
XLA Ops:
  7.2 0.0 all-gather.3.cloned.1.call-start
  7.3 11.5 %copy.21 = f32[256,16,512]{2,0,1:T(8,128)} copy(f32[256,16,512]{2,1,0:T(8,128)} %param.7) | data formatting | bytes 16777216 | tf_op args[0]
  18.8 1.8 dynamic-slice_bitcast_fusion
  20.6 0.1 fusion.12
  20.7 4.9 %collective-permute-start = (f32[3,64,512]{2,1,0:T(8,128)S(1)}, f32[3,64,512]{2,1,0:T(8,128)S(1)}, u32[]{:S(2)}, u32[]{:S(2)}) collective-permute-start(f32[3,64,512]{2,1,0:T(8,128)S(1)} %get-tuple-element.16), channel_id=1, source_target_pairs={{0,1},{1,2},{2,3},{3,4},{4,5},{5,6},{6,7},{8,9},{9,10},{10,11},{11... | collective-permute-start | bytes 1179656 | tf_op jit(solution)/shard_map/ppermute | solution.py:232
  25.6 1.3 collective-permute-start.1
  26.9 15.5 %collective-permute-done = f32[3,64,512]{2,1,0:T(8,128)S(1)} collective-permute-done((f32[3,64,512]{2,1,0:T(8,128)S(1)}, f32[3,64,512]{2,1,0:T(8,128)S(1)}, u32[]{:S(2)}, u32[]{:S(2)}) %collective-permute-start) | collective-permute-done | bytes 393248 | tf_op jit(solution)/shard_map/ppermute | solution.py:232
  42.3 1.0 pad_maximum_fusion
  43.4 0.0 all-gather.3.cloned.1.call-update
  43.4 0.0 all-reduce.6.cloned.1.call-start
  43.5 4.4 %collective-permute-start.2 = (f32[4,3,512]{2,1,0:T(4,128)S(1)}, f32[4,3,512]{2,1,0:T(4,128)S(1)}, u32[]{:S(2)}, u32[]{:S(2)}) collective-permute-start(f32[4,3,512]{2,1,0:T(4,128)S(1)} %get-tuple-element.21), channel_id=1, source_target_pairs={{0,1},{1,2},{2,3},{3,4},{4,5},{5,6},{6,7},{8,9},{9,10},{10,11},{11... | collective-permute-start | bytes 73736 | tf_op jit(solution)/shard_map/ppermute | solution.py:232
  47.9 1.3 collective-permute-start.3
  49.3 0.6 fusion
  49.9 3.9 %copy-done = f32[256,16,512]{2,0,1:T(8,128)S(1)} copy-done((f32[256,16,512]{2,0,1:T(8,128)S(1)}, f32[256,16,512]{2,0,1:T(8,128)}, u32[]{:S(2)}) %copy-start) | copy-done | bytes 8388632
  53.8 7.2 %obs_info.1 = (f32[256,256]{1,0:T(8,128)S(1)}, f32[256,128]{1,0:T(8,128)S(1)}) custom-call(f32[16,256,512]{2,1,0:T(8,128)S(1)} %bitcast.37, f32[16,512]{1,0:T(8,128)S(1)} %get-tuple-element.24.counts_ref, f32[16,512]{1,0:T(8,128)S(1)} %get-tuple-element.23.weights_ref), custom_call_target="tpu_custom_call" | custom-call | flops 3221225472 | bytes 8388608 | tf_op jit(solution)/shard_map/obs_info/pallas_call | solution.py:288
  61.0 0.1 slice.97
  61.1 0.1 reduce_sum.18
  61.4 0.1 slice_select_fusion
  61.5 0.1 bitcast_dynamic-update-slice_fusion
  61.7 12.5 %all-gather.3.cloned.1.call-done.halo_ref = f32[6,256,512]{2,1,0:T(8,128)} async-done(((f32[6,64,512]{2,1,0:T(8,128)}), f32[6,256,512]{2,1,0:T(8,128)}) %all-gather.3.cloned.1.call-update) | async-done | bytes 3145744 | tf_op jit(solution)/shard_map/all_gather | solution.py:255
  74.2 1.9 copy-done.1
  76.1 38.0 %propagate.1 = f32[256,256]{1,0:T(8,128)S(1)} custom-call(f32[16,256,512]{2,1,0:T(8,128)} %bitcast.36, f32[6,256,512]{2,1,0:T(8,128)S(1)} %copy-done.1, f32[5,20,512]{2,1,0:T(8,128)S(1)} %slice.94.fg_ref, f32[5,20,512]{2,1,0:T(8,128)S(1)} %slice.101.lg_ref), custom_call_target="tpu_custom_call" | custom-call | flops 138412032 | bytes 8388608 | tf_op jit(solution)/shard_map/propagate/pallas_call | solution.py:307
  114.1 0.8 maximum_bitcast_fusion
  114.9 0.0 all-reduce.6.cloned.1.call-update
  114.9 0.0 all-gather.5.cloned.1.call-start
  115.0 72.5 %all-reduce.6.cloned.1.call-done = f32[1,513,256]{2,1,0:T(8,128)} async-done(((f32[1,513,256]{2,1,0:T(8,128)}), f32[1,513,256]{2,1,0:T(8,128)}) %all-reduce.6.cloned.1.call-update) | async-done | bytes 525328 | tf_op jit(solution)/shard_map/psum | solution.py:325
  187.5 23.6 %all-gather.5.cloned.1.call-done = f32[4,513,256]{2,1,0:T(8,128)} async-done(((f32[1,513,256]{2,1,0:T(8,128)}), f32[4,513,256]{2,1,0:T(8,128)}) %all-gather.5.cloned.1.call-update) | async-done | bytes 2101264 | tf_op jit(solution)/shard_map/all_gather | solution.py:326
  211.1 0.8 slice.106
  211.9 1.7 fusion.11
  213.6 39.5 %join.1 = f32[5,256]{1,0:T(8,128)S(1)} custom-call(f32[4,256,256]{2,1,0:T(8,128)S(1)} %get-tuple-element.15.prop_ref, f32[4,256,256]{2,1,0:T(8,128)S(1)} %get-tuple-element.14.info_ref, f32[4,256]{1,0:T(4,128)S(1)} %bitcast.38), custom_call_target="tpu_custom_call" | custom-call | tf_op jit(solution)/shard_map/join/pallas_call | solution.py:327
  253.0 0.6 dynamic-slice_bitcast_fusion.1
  253.6 4.6 %multiply_reduce_fusion = f32[16,512]{1,0:T(8,128)} fusion(f32[256,16,512]{2,1,0:T(8,128)} %param.7, f32[256]{0:T(256)S(1)} %bitcast.43), kind=kLoop, calls=%fused_computation | loop fusion | flops 4186112 | bytes 8422400 | tf_op jit(solution)/shard_map/reduce_sum | solution.py:339
  (43 shorter events, 0.4 us)
Async XLA Ops:
  7.2 67.0 %all-gather.3.cloned.1.call-start = ((), (), s32[]{:S(2)}) async-start(), calls=%async_computation | async-start | bytes 3932160 | tf_op jit(solution)/shard_map/all_gather | solution.py:255
  7.2 36.2 %copy-start.5 = (s32[16,512]{1,0:T(8,128)S(1)}, s32[16,512]{1,0:T(8,128)}, u32[]{:S(2)}) copy-start(s32[16,512]{1,0:T(8,128)} %param.11) | copy-start | bytes 98308
  7.2 36.2 %copy-start.2 = (f32[1,16,512]{2,1,0:T(8,128)S(1)}, f32[1,16,512]{2,1,0:T(8,128)}, u32[]{:S(2)}) copy-start(f32[1,16,512]{2,1,0:T(8,128)} %param.10) | copy-start | bytes 98308
  7.2 36.2 %copy-start.3 = (f32[1,16,512]{2,1,0:T(8,128)S(1)}, f32[1,16,512]{2,1,0:T(8,128)}, u32[]{:S(2)}) copy-start(f32[1,16,512]{2,1,0:T(8,128)} %param.9) | copy-start | bytes 98308
  7.2 36.2 %copy-start.4 = (f32[1,16,512]{2,1,0:T(8,128)S(1)}, f32[1,16,512]{2,1,0:T(8,128)}, u32[]{:S(2)}) copy-start(f32[1,16,512]{2,1,0:T(8,128)} %param.8) | copy-start | bytes 98308
  18.8 30.4 %copy-start.7 = (s32[1,512]{1,0:T(1,128)S(1)}, s32[1,512]{1,0:T(1,128)}, u32[]{:S(2)}) copy-start(s32[1,512]{1,0:T(1,128)} %param.12) | copy-start | bytes 6148
  18.8 30.5 %copy-start.6 = (f32[1,512]{1,0:T(1,128)S(1)}, f32[1,512]{1,0:T(1,128)}, u32[]{:S(2)}) copy-start(f32[1,512]{1,0:T(1,128)} %param.13) | copy-start | bytes 6148
  20.7 21.7 %collective-permute-start = (f32[3,64,512]{2,1,0:T(8,128)S(1)}, f32[3,64,512]{2,1,0:T(8,128)S(1)}, u32[]{:S(2)}, u32[]{:S(2)}) collective-permute-start(f32[3,64,512]{2,1,0:T(8,128)S(1)} %get-tuple-element.16), channel_id=1, source_target_pairs={{0,1},{1,2},{2,3},{3,4},{4,5},{5,6},{6,7},{8,9},{9,10},{10,11},{11... | collective-permute-start | bytes 1179656 | tf_op jit(solution)/shard_map/ppermute | solution.py:232
  25.6 16.8 %collective-permute-start.1 = (f32[3,64,512]{2,1,0:T(8,128)S(1)}, f32[3,64,512]{2,1,0:T(8,128)S(1)}, u32[]{:S(2)}, u32[]{:S(2)}) collective-permute-start(f32[3,64,512]{2,1,0:T(8,128)S(1)} %get-tuple-element.17), channel_id=1, source_target_pairs={{1,0},{2,1},{3,2},{4,3},{5,4},{6,5},{7,6},{9,8},{10,9},{11,10},{12... | collective-permute-start | bytes 1179656 | tf_op jit(solution)/shard_map/ppermute | solution.py:233
  43.4 144.1 %all-reduce.6.cloned.1.call-start = ((), (), s32[]{:S(2)}) async-start(), calls=%async_computation.1 | async-start | bytes 1064960 | tf_op jit(solution)/shard_map/psum | solution.py:325
  43.5 17.7 %collective-permute-start.2 = (f32[4,3,512]{2,1,0:T(4,128)S(1)}, f32[4,3,512]{2,1,0:T(4,128)S(1)}, u32[]{:S(2)}, u32[]{:S(2)}) collective-permute-start(f32[4,3,512]{2,1,0:T(4,128)S(1)} %get-tuple-element.21), channel_id=1, source_target_pairs={{0,1},{1,2},{2,3},{3,4},{4,5},{5,6},{6,7},{8,9},{9,10},{10,11},{11... | collective-permute-start | bytes 73736 | tf_op jit(solution)/shard_map/ppermute | solution.py:232
  47.9 13.3 %collective-permute-start.3 = (f32[4,3,512]{2,1,0:T(4,128)S(1)}, f32[4,3,512]{2,1,0:T(4,128)S(1)}, u32[]{:S(2)}, u32[]{:S(2)}) collective-permute-start(f32[4,3,512]{2,1,0:T(4,128)S(1)} %get-tuple-element.22), channel_id=1, source_target_pairs={{1,0},{2,1},{3,2},{4,3},{5,4},{6,5},{7,6},{9,8},{10,9},{11,10},{12... | collective-permute-start | bytes 73736 | tf_op jit(solution)/shard_map/ppermute | solution.py:233
  49.9 3.9 %copy-start = (f32[256,16,512]{2,0,1:T(8,128)S(1)}, f32[256,16,512]{2,0,1:T(8,128)}, u32[]{:S(2)}) copy-start(f32[256,16,512]{2,0,1:T(8,128)} %copy.21) | copy-start | bytes 25165828
  74.2 1.9 copy-start.1
  114.9 96.2 %all-gather.5.cloned.1.call-start = ((), (), s32[]{:S(2)}) async-start(), calls=%async_computation.2 | async-start | bytes 2662400 | tf_op jit(solution)/shard_map/all_gather | solution.py:326
Sparse Core Ops, SparseCore 0:
  43.5 30.6 all-gather.2
  115.1 72.3 all-reduce.5
  189.1 21.9 all-gather.4

commit v2 on v1

--- a/solution.py
+++ b/solution.py
@@ -33,30 +33,228 @@
     )
 
 
-def obs_kernel(rows, basis_ref, counts_ref, weights_ref, info_ref, rhs_ref):
+def dot3(a, b):
+    ah, al = split(a)
+    bh, bl = split(b)
+    return dot16(ah, bh, NN) + dot16(ah, bl, NN) + dot16(al, bh, NN)
+
+
+MESH = pl.DeviceIdType.MESH
+
+
+def remote(src, dst, send, recv, **where):
+    return pltpu.make_async_remote_copy(
+        src_ref=src, dst_ref=dst, send_sem=send, recv_sem=recv, device_id=where, device_id_type=MESH
+    )
+
+
+def edge_kernel(
+    chips, tiles, basis_ref, cells_ref, counts_ref, weights_ref, halo_ref, fringe_ref, info_ref,
+    rhs_ref, edge, xh, xl, first_send, first_recv, cell_send, cell_recv, over_send, over_recv,
+    mate_send, mate_recv,
+):
+    width, rows, columns = basis_ref.shape
+    group, tile = lax.axis_index("tm"), lax.axis_index("tile")
+    chip, core = group // 2, group % 2
+    mate = group + 1 - 2 * core
+    share = edge.shape[1]
+    mine = pl.multiple_of(group * share, share)
+    others = [((chip + i) % chips) * 2 + core for i in range(1, chips)]
+    has = (tile > 0, tile < tiles - 1)
+    near = (tile - 1, tile + 1)
+
+    barrier = pltpu.get_barrier_semaphore()
+    for peer in others + [mate]:
+        pl.semaphore_signal(barrier, inc=1, device_id={"tm": peer}, device_id_type=MESH)
+    for peer in ((tile + tiles - 1) % tiles, (tile + 1) % tiles):
+        pl.semaphore_signal(barrier, inc=1, device_id={"tile": peer}, device_id_type=MESH)
+
+    def cut(j, _):
+        x = basis_ref[pl.ds(mine + 8 * j, 8)]
+        y = jnp.swapaxes(x, 0, 1)
+        k = pl.multiple_of(8 * j, 8)
+        edge[:HALF, pl.ds(k, 8), :] = y[:HALF]
+        edge[HALF:, pl.ds(k, 8), :] = y[rows - HALF :]
+        return 0
+
+    lax.fori_loop(0, share // 8, cut, 0)
+    pl.semaphore_wait(barrier, chips + 2)
+
+    def part(side, k):
+        return halo_ref.at[pl.ds(side * HALF, HALF), pl.ds(pl.multiple_of(k, share), share), :]
+
+    def send(side):
+        other = 1 - side
+        first = 0 if side == 0 else rows - HALF
+        return (
+            remote(edge.at[pl.ds(side * HALF, HALF)], part(other, mine), first_send.at[side],
+                   first_recv.at[other], tile=near[side]),
+            remote(cells_ref.at[pl.ds(first, HALF)], fringe_ref.at[pl.ds(other * HALF, HALF)],
+                   cell_send.at[side], cell_recv.at[other], tile=near[side]),
+        )
+
+    def arrival(side):
+        return (
+            remote(edge.at[pl.ds(side * HALF, HALF)], part(side, mine), first_send.at[side],
+                   first_recv.at[side], tile=near[side]),
+            remote(cells_ref.at[pl.ds(0, HALF)], fringe_ref.at[pl.ds(side * HALF, HALF)],
+                   cell_send.at[side], cell_recv.at[side], tile=near[side]),
+        )
+
+    def over(side, i):
+        return remote(part(side, mine), part(side, mine), over_send.at[side, i],
+                      over_recv.at[side, i], tm=others[i])
+
+    def to_mate(side, i):
+        k = (((chip - i + chips) % chips) * 2 + core) * share
+        return remote(part(side, k), part(side, k), mate_send.at[side, i], mate_recv.at[side, i],
+                      tm=mate)
+
+    for side in range(2):
+
+        @pl.when(has[side])
+        def _():
+            for copy in send(side):
+                copy.start()
+
+        @pl.when(jnp.logical_not(has[side]))
+        def _():
+            halo_ref[side * HALF : (side + 1) * HALF] = jnp.zeros(
+                (HALF, width, columns), jnp.float32
+            )
+            fringe_ref[side * HALF : (side + 1) * HALF] = jnp.zeros(
+                (HALF,) + fringe_ref.shape[1:], jnp.float32
+            )
+
+    def turn(j, _):
+        k = pl.multiple_of(16 * j, 16)
+        y = jnp.swapaxes(basis_ref[pl.ds(k, 16)], 0, 1)
+        high, low = split(y)
+        xh[:, pl.ds(k, 16), :] = high
+        xl[:, pl.ds(k, 16), :] = low
+        return 0
+
+    lax.fori_loop(0, width // 16, turn, 0)
     info_ref[...] = jnp.zeros_like(info_ref)
     rhs_ref[...] = jnp.zeros_like(rhs_ref)
 
     def row(r, _):
-        x = basis_ref[r]
-        y = x * counts_ref[pl.ds(r, 1), :]
+        a, b = xh[r], xl[r]
+        x = a.astype(jnp.float32) + b.astype(jnp.float32)
+        yh, yl = split(x * counts_ref[pl.ds(r, 1), :])
         z = x * weights_ref[pl.ds(r, 1), :]
-        xh, xl = split(x)
-        yh, yl = split(y)
-        info_ref[...] += dot16(xh, yh, NT) + dot16(xh, yl, NT) + dot16(xl, yh, NT)
-        part = z[:, :128]
-        for c in range(128, z.shape[1], 128):
-            part += z[:, c : c + 128]
-        rhs_ref[...] += part
+        info_ref[...] += dot16(a, yh, NT) + dot16(a, yl, NT) + dot16(b, yh, NT)
+        part_sum = z[:, :128]
+        for c in range(128, columns, 128):
+            part_sum += z[:, c : c + 128]
+        rhs_ref[...] += part_sum
         return 0
 
-    lax.fori_loop(0, rows, row, 0)
+    lax.fori_loop(0, rows // 2, row, 0)
+    for side in range(2):
+
+        @pl.when(has[side])
+        def _():
+            arrival(side)[0].wait_recv()
+            for i in range(chips - 1):
+                over(side, i).start()
+            to_mate(side, 0).start()
+
+    lax.fori_loop(rows // 2, rows, row, 0)
+    for side in range(2):
+
+        @pl.when(has[side])
+        def _():
+            for i in range(chips - 1):
+                over(side, i).wait_recv()
+                to_mate(side, i + 1).start()
+
+    for side in range(2):
+
+        @pl.when(has[side])
+        def _():
+            for i in range(chips):
+                to_mate(side, i).wait_recv()
+                to_mate(side, i).wait_send()
+            for i in range(chips - 1):
+                over(side, i).wait_send()
+            arrival(side)[1].wait_recv()
+            for copy in send(side):
+                copy.wait_send()
+
+
+def spread_kernel(chips, tiles, part_ref, out_ref, land, s1, r1, s2, r2, s3, r3, s4, r4):
+    rows = part_ref.shape[0] // tiles
+    group, tile = lax.axis_index("tm"), lax.axis_index("tile")
+    chip, core = group // 2, group % 2
+    mate = group + 1 - 2 * core
+    others = [((chip + i) % chips) * 2 + core for i in range(1, chips)]
+    far = [(tile + d) % tiles for d in range(1, tiles)]
+
+    barrier = pltpu.get_barrier_semaphore()
+    for peer in others + [mate]:
+        pl.semaphore_signal(barrier, inc=1, device_id={"tm": peer}, device_id_type=MESH)
+    for peer in far:
+        pl.semaphore_signal(barrier, inc=1, device_id={"tile": peer}, device_id_type=MESH)
+    pl.semaphore_wait(barrier, chips + tiles - 1)
+
+    def lines(t):
+        return pl.ds(pl.multiple_of(t * rows, rows), rows)
+
+    def slot(g, t):
+        return out_ref.at[g, lines(t), :]
+
+    def scatter(d):
+        return remote(part_ref.at[lines(far[d]), :], land.at[d], s1.at[d], r1.at[d], tile=far[d])
+
+    def gather(d):
+        return remote(slot(group, tile), slot(group, tile), s2.at[d], r2.at[d], tile=far[d])
+
+    def held(d):
+        return (tile - d + tiles) % tiles
+
+    def over(d, i):
+        place = slot(group, held(d))
+        return remote(place, place, s3.at[d, i], r3.at[d, i], tm=others[i])
+
+    def to_mate(d, i):
+        place = slot(((chip - i + chips) % chips) * 2 + core, held(d))
+        return remote(place, place, s4.at[d, i], r4.at[d, i], tm=mate)
+
+    for d in range(tiles - 1):
+        scatter(d).start()
+    total = part_ref[lines(tile), :]
+    for d in range(tiles - 1):
+        scatter(d).wait_recv()
+        total = total + land[d]
+    out_ref[group, lines(tile), :] = total
+    for d in range(tiles - 1):
+        gather(d).start()
+    for d in range(tiles):
+        if d:
+            gather(d - 1).wait_recv()
+        for i in range(chips - 1):
+            over(d, i).start()
+        to_mate(d, 0).start()
+    for d in range(tiles):
+        for i in range(chips - 1):
+            over(d, i).wait_recv()
+            to_mate(d, i + 1).start()
+    for d in range(tiles):
+        for i in range(chips):
+            to_mate(d, i).wait_recv()
+            to_mate(d, i).wait_send()
+        for i in range(chips - 1):
+            over(d, i).wait_send()
+    for d in range(tiles - 1):
+        scatter(d).wait_send()
+        gather(d).wait_send()
 
 
 def stencil_kernel(
-    rows, block, basis_ref, halo_ref, fg_ref, lg_ref, prop_ref, gf, gl, f1, l1, f2, l2, fh, fl, lh, ll
+    rows, block, basis_ref, halo_ref, fg_ref, lg_ref, prop_ref, turned, gf, gl, f1, l1, f2, l2, fh, fl, lh, ll
 ):
-    width, columns = basis_ref.shape[1:]
+    width, _, columns = basis_ref.shape
     halves = block // 8
     for which, (src, dst) in enumerate(((fg_ref, gf), (lg_ref, gl))):
         for i in range(5):
@@ -79,8 +277,10 @@
                 return halo_ref[r + HALF, pl.ds(k + 8 * h, 8), :]
             if r >= rows:
                 return halo_ref[r - rows + HALF, pl.ds(k + 8 * h, 8), :]
-            return basis_ref[r, pl.ds(k + 8 * h, 8), :]
-
+            return turned[r, h]
+
+        for h in range(halves):
+            turned[:, h] = jnp.swapaxes(basis_ref[pl.ds(k + 8 * h, 8)], 0, 1)
         edge = HALF - 1
         before = [load(-edge - 1, h) for h in range(halves)]
         here = [load(-edge, h) for h in range(halves)]
@@ -143,7 +343,31 @@
         x[...] = scale * (eye + r)
         size = jnp.maximum(size, jnp.sum(r * r))
 
+    def small(c):
+        return jnp.logical_not(c[1] <= 1e-4) & (c[0] < 30)
+
     def grow(carry):
+        it, _ = carry
+        size = 0.0
+        for x, t in zip(invs, tmps):
+            r = t[...].astype(jnp.bfloat16)
+            r = dot16(r, r, NN)
+            t[...] = r
+            x[...] += dot16(x[...].astype(jnp.bfloat16), r.astype(jnp.bfloat16), NN)
+            size = jnp.maximum(size, jnp.sum(r * r))
+        return it + 1, size
+
+    lax.while_loop(small, grow, (0, size))
+
+    def residual():
+        size = 0.0
+        for a, x, t in zip(mats, invs, tmps):
+            r = eye - dot32(a[...], x[...])
+            t[...] = r
+            size = jnp.maximum(size, jnp.sum(r * r))
+        return size
+
+    def grow_exact(carry):
         it, _ = carry
         size = 0.0
         for x, t in zip(invs, tmps):
@@ -153,18 +377,29 @@
             size = jnp.maximum(size, jnp.sum(r * r))
         return it + 1, size
 
-    lax.while_loop(lambda c: (c[1] > 1e-4) & (c[0] < 30), grow, (0, size))
+    def again(_):
+        size = 0.0
+        for a, x, t in zip(mats, invs, tmps):
+            scale = 1.0 / jnp.max(jnp.sum(jnp.abs(a[...]), axis=0, keepdims=True))
+            r = eye - scale * a[...]
+            t[...] = r
+            x[...] = scale * (eye + r)
+            size = jnp.maximum(size, jnp.sum(r * r))
+        lax.while_loop(small, grow_exact, (0, size))
+        return residual()
+
+    size = residual()
+    size = lax.cond(size <= 0.25, lambda v: v, again, size)
 
     def correct(carry):
         it, _ = carry
-        size = 0.0
-        for a, x in zip(mats, invs):
-            r = eye - dot32(a[...], x[...])
-            x[...] += dot32(x[...], r)
-            size = jnp.maximum(size, jnp.sum(r * r))
-        return it + 1, size
-
-    lax.while_loop(lambda c: (c[1] > 1e-7) & (c[0] < 5), correct, (0, jnp.float32(1.0)))
+        for x, t in zip(invs, tmps):
+            x[...] += dot3(x[...], t[...])
+        return it + 1, residual()
+
+    lax.while_loop(lambda c: (c[1] > 1e-6) & (c[0] < 6), correct, (0, size))
+    for x, t in zip(invs, tmps):
+        x[...] += dot3(x[...], t[...])
 
 
 def join_kernel(groups, scale_prop, scale_obs, prop_ref, info_ref, rhs_ref, out_ref, s, x, t, w):
@@ -224,16 +459,6 @@
 VMEM = pltpu.VMEM
 
 
-def shift(cells, width, dim):
-    count = lax.axis_size("tile")
-    head = lax.slice_in_dim(cells, 0, width, axis=dim)
-    tail = lax.slice_in_dim(cells, cells.shape[dim] - width, cells.shape[dim], axis=dim)
-    return (
-        lax.ppermute(tail, "tile", [(i, i + 1) for i in range(count - 1)]),
-        lax.ppermute(head, "tile", [(i + 1, i) for i in range(count - 1)]),
-    )
-
-
 def moved(x, by, dim):
     zero = jnp.zeros_like(lax.slice_in_dim(x, 0, 1, axis=dim))
     if by > 0:
@@ -248,29 +473,11 @@
     tiles = lax.axis_size("tile")
     group = lax.axis_index("tm")
 
-    share = width // groups
-    by_row = basis.transpose(1, 0, 2)
-    mine = lax.dynamic_slice_in_dim(by_row, group * share, share, axis=1)
-    above, below = shift(mine, HALF, 0)
-    halo = lax.all_gather(jnp.concatenate([above, below], axis=0), "tm", axis=1, tiled=True)
-
+    chips = groups // 2
+    zeros = jnp.zeros_like(diffusion[0])
     cells = jnp.stack(
-        [diffusion[0], drift_x[0], drift_y[0], land_sea.astype(jnp.float32)], axis=0
+        [diffusion[0], drift_x[0], drift_y[0], land_sea.astype(jnp.float32)] + [zeros] * 4, axis=1
     )
-    before, after = shift(cells, HALF, 1)
-    cells = jnp.concatenate([before, cells, after], axis=1)
-    d, dx, dy, sea = cells[0], cells[1], cells[2], cells[3]
-    column = lax.broadcasted_iota(jnp.int32, d.shape, 1)
-    center = sea * (1.0 - 4.0 * d)
-    east = sea * (d * (1.0 - dx))
-    west = sea * (d * (1.0 + dx))
-    north = jnp.where(column == columns - 1, 0.0, sea * (d * (1.0 - dy)))
-    south = jnp.where(column == 0, 0.0, sea * (d * (1.0 + dy)))
-    forward = jnp.stack([center, east, west, north, south])[:, 1:-1]
-    backward = jnp.stack(
-        [center, moved(west, 1, 0), moved(east, -1, 0), moved(south, 1, 1), moved(north, -1, 1)]
-    )[:, 1:-1]
-
     offset = lax.axis_index("tile") * (rows * columns)
     local = obs_cells[0] - offset
     inside = (local >= 0) & (local < rows * columns)
@@ -285,22 +492,44 @@
     )
     hits = dot32(hits, in_col, NT)
 
-    info, rhs = pl.pallas_call(
-        functools.partial(obs_kernel, rows),
+    share = width // groups
+    DMA = pltpu.SemaphoreType.DMA
+    whole = pl.BlockSpec(memory_space=VMEM)
+    halo, fringe, info, rhs = pl.pallas_call(
+        functools.partial(edge_kernel, chips, tiles),
         out_shape=(
+            jax.ShapeDtypeStruct((2 * HALF, width, columns), jnp.float32),
+            jax.ShapeDtypeStruct((2 * HALF, 8, columns), jnp.float32),
             jax.ShapeDtypeStruct((width, width), jnp.float32),
             jax.ShapeDtypeStruct((width, 128), jnp.float32),
         ),
-        in_specs=[pl.BlockSpec(memory_space=VMEM)] * 3,
-        out_specs=[pl.BlockSpec(memory_space=VMEM)] * 2,
-        compiler_params=pltpu.CompilerParams(vmem_limit_bytes=32 << 20),
-        cost_estimate=pl.CostEstimate(
-            flops=6 * width * width * rows * columns,
-            bytes_accessed=4 * width * rows * columns,
-            transcendentals=0,
+        in_specs=[whole] * 4,
+        out_specs=[whole] * 4,
+        scratch_shapes=[VMEM((2 * HALF, share, columns), jnp.float32)]
+        + [VMEM((rows, width, columns), jnp.bfloat16)] * 2
+        + [DMA((2,))] * 4
+        + [DMA((2, max(chips - 1, 1)))] * 2
+        + [DMA((2, chips))] * 2,
+        compiler_params=pltpu.CompilerParams(
+            vmem_limit_bytes=40 << 20, collective_id=0, has_side_effects=True
         ),
-        name="obs_info",
-    )(by_row, hits[:rows], hits[rows:])
+        name="edges",
+    )(basis, cells, hits[:rows], hits[rows:])
+    info = jnp.concatenate([info, jnp.broadcast_to(jnp.sum(rhs, axis=1)[None, :], (8, width))])
+    info = lax.all_gather(lax.psum(info, "tile"), "tm", axis=0)
+
+    cells = jnp.concatenate([fringe[:HALF], cells, fringe[HALF:]], axis=0)
+    d, dx, dy, sea = cells[:, 0], cells[:, 1], cells[:, 2], cells[:, 3]
+    column = lax.broadcasted_iota(jnp.int32, d.shape, 1)
+    center = sea * (1.0 - 4.0 * d)
+    east = sea * (d * (1.0 - dx))
+    west = sea * (d * (1.0 + dx))
+    north = jnp.where(column == columns - 1, 0.0, sea * (d * (1.0 - dy)))
+    south = jnp.where(column == 0, 0.0, sea * (d * (1.0 + dy)))
+    forward = jnp.stack([center, east, west, north, south])[:, 1:-1]
+    backward = jnp.stack(
+        [center, moved(west, 1, 0), moved(east, -1, 0), moved(south, 1, 1), moved(north, -1, 1)]
+    )[:, 1:-1]
 
     block = 16
     edge_rows = rows + 2 * (HALF - 1)
@@ -309,21 +538,33 @@
         out_shape=jax.ShapeDtypeStruct((width, width), jnp.float32),
         in_specs=[pl.BlockSpec(memory_space=VMEM)] * 4,
         out_specs=pl.BlockSpec(memory_space=VMEM),
-        scratch_shapes=[VMEM((5, edge_rows, 8, columns), jnp.float32)] * 2
+        scratch_shapes=[VMEM((rows, block // 8, 8, columns), jnp.float32)]
+        + [VMEM((5, edge_rows, 8, columns), jnp.float32)] * 2
         + [VMEM((edge_rows, block // 8, 8, columns), jnp.float32)] * 4
         + [VMEM((rows, width, columns), jnp.bfloat16)] * 4,
         compiler_params=pltpu.CompilerParams(vmem_limit_bytes=48 << 20),
         cost_estimate=pl.CostEstimate(
-            flops=66 * width * rows * columns,
+            flops=20000 * width * rows * columns,
             bytes_accessed=4 * width * rows * columns,
             transcendentals=0,
         ),
         name="propagate",
-    )(by_row, halo, forward, backward)
-
-    packed = jnp.concatenate([prop, info, jnp.sum(rhs, axis=1)[None, :]], axis=0)
-    packed = lax.psum(packed, "tile")
-    packed = lax.all_gather(packed, "tm", axis=0)
+    )(basis, halo, forward, backward)
+
+    props = pl.pallas_call(
+        functools.partial(spread_kernel, chips, tiles),
+        out_shape=jax.ShapeDtypeStruct((groups, width, width), jnp.float32),
+        in_specs=[whole],
+        out_specs=whole,
+        scratch_shapes=[VMEM((tiles - 1, width // tiles, width), jnp.float32)]
+        + [DMA((tiles - 1,))] * 4
+        + [DMA((tiles, max(chips - 1, 1)))] * 2
+        + [DMA((tiles, chips))] * 2,
+        compiler_params=pltpu.CompilerParams(
+            vmem_limit_bytes=16 << 20, collective_id=1, has_side_effects=True
+        ),
+        name="spread",
+    )(prop)
     states = pl.pallas_call(
         functools.partial(
             join_kernel, groups, 1.0 / (rows * columns * tiles), 1.0 / nobs
@@ -334,7 +575,7 @@
         scratch_shapes=[VMEM((groups + 1, width, width), jnp.float32)] * 4,
         compiler_params=pltpu.CompilerParams(vmem_limit_bytes=48 << 20),
         name="join",
-    )(packed[:, :width], packed[:, width : 2 * width], packed[:, 2 * width])
+    )(props, info[:, :width], info[:, width])
     coeffs = lax.dynamic_slice_in_dim(states, group, 2, axis=0)
     end_fields = jnp.sum(coeffs[1][:, None, None] * basis, axis=0)
     return coeffs[None], end_fields[None]

time: 265 us -> 232 us (0.88)
  waiting for transfers between devices: 124 us -> 86.3 us
  Pallas kernels: 84.6 us -> 110 us
  starting transfers between devices: 12 us -> 0.08 us
  local copies, waits for them, and re-layouts: 22.5 us -> 12.4 us
    pallas_call x1 -> x2, Pallas kernels: 7.17 us -> 44.9 us  [the longest x1 24.6 us: shards(): pl.pallas_call(functools.partial(edge_kernel, chips, tiles), out_shape=(j...]
    all_gather x2 -> x1, waiting for transfers between devices: 36.2 us -> 0.02 us  [shards(): info = lax.all_gather(lax.psum(info, 'tile'), 'tm', axis=0)]
    ppermute x4 -> x0, waiting for transfers between devices: 15.5 us -> none  [the longest x2 15.5 us: shift(): lax.ppermute(tail, 'tile', [(i, i + 1) for i in range(count - 1)])]
    psum x1, waiting for transfers between devices: 72.5 us -> 86.2 us  [shards(): info = lax.all_gather(lax.psum(info, 'tile'), 'tm', axis=0)]
    pallas_call x1, Pallas kernels: 39.5 us -> 25.7 us  [shards(): pl.pallas_call(functools.partial(join_kernel, groups, 1.0 / (rows * colum...]
    ppermute x4 -> x0, starting transfers between devices: 11.9 us -> none  [the longest x2 9.28 us: shift(): lax.ppermute(tail, 'tile', [(i, i + 1) for i in range(count - 1)])]
    unnamed x22 -> x14, local copies, waits for them, and re-layouts: 17.3 us -> 9.23 us
  transfers between devices with their start and end apart: 7 -> 2, of which waited for: 4 -> 1; matrix products, arithmetic and copies ran while one was open for 0% -> 0% of each run, Pallas kernels for 3% -> 26%
where the time goes in v2:
time: 232 us; the launch traced here: 231 us
  Pallas kernels  110 us (47%)
  waiting for transfers between devices  86.3 us (37%)
  between operations  14.3 us (6%)
  local copies, waits for them, and re-layouts  12.4 us (5%)
  other arithmetic  7.83 us (3%)
    psum x1, waiting for transfers between devices, shards(): info = lax.all_gather(lax.psum(info, 'tile'), 'tm', axis=0)  86.2 us
    pallas_call x1, Pallas kernels, shards(): pl.pallas_call(functools.partial(stencil_kernel, rows, block), out_shape=...  39.2 us
    pallas_call x1, Pallas kernels, shards(): pl.pallas_call(functools.partial(join_kernel, groups, 1.0 / (rows * colum...  25.7 us
    pallas_call x1, Pallas kernels, shards(): pl.pallas_call(functools.partial(edge_kernel, chips, tiles), out_shape=(j...  24.6 us
    pallas_call x1, Pallas kernels, shards(): pl.pallas_call(functools.partial(spread_kernel, chips, tiles), out_shape=...  20.4 us
    unnamed x14, local copies, waits for them, and re-layouts  9.23 us
  transfers between devices with their start and end apart: 2, of which 1 were waited for; matrix products, arithmetic and copies ran while one was open for 0% of the time, Pallas kernels for 26%

profile of v2, /device:TPU:0, one launch (start us, length us, event | category | flops | bytes accessed | tf_op | source)
XLA Modules:
  0.0 231.4 jit_solution(14703579352928154540)
XLA Ops:
  7.2 0.0 all-reduce.6.cloned.1.call-start
  7.2 0.8 constant_dynamic-update-slice_fusion.3
  8.0 0.8 constant_dynamic-update-slice_fusion.2
  8.7 0.8 constant_dynamic-update-slice_fusion.1
  9.5 0.8 constant_dynamic-update-slice_fusion
  10.3 0.2 copy.13.cells_ref
  10.4 0.7 and_select_fusion.2
  11.2 0.7 fusion.7
  11.9 0.6 fusion
  12.5 0.0 copy-start
  12.5 3.4 %copy-done = f32[256,16,512]{2,1,0:T(8,128)S(1)} copy-done((f32[256,16,512]{2,1,0:T(8,128)S(1)}, f32[256,16,512]{2,1,0:T(8,128)}, u32[]{:S(2)}) %copy-start) | copy-done | bytes 8388632
  15.9 24.6 %edges.1 = (f32[6,256,512]{2,1,0:T(8,128)S(1)}, f32[6,8,512]{2,1,0:T(8,128)S(1)}, f32[256,256]{1,0:T(8,128)S(1)}, f32[256,128]{1,0:T(8,128)S(1)}) custom-call(f32[256,16,512]{2,1,0:T(8,128)S(1)} %copy-done, f32[16,8,512]{2,1,0:T(8,128)S(1)} %copy.13.cells_ref, f32[16,512]{1,0:T(8,128)S(1)} %get-tuple-element.24.counts_ref, ...), custom_call_target="tpu_custom_call" | custom-call | tf_op jit(solution)/shard_map/edges/pallas_call | solution.py:498
  40.5 1.6 copy-done.1
  42.1 0.1 reduce_sum.18
  42.2 0.7 maximum_bitcast_fusion
  42.9 0.0 all-reduce.6.cloned.1.call-update
  43.0 0.0 all-gather.2.cloned.1.call-start
  43.0 0.1 copy.14
  43.3 0.1 slice.83
  43.5 0.1 slice_select_fusion.1
  43.6 0.1 bitcast_dynamic-update-slice_fusion
  43.7 86.2 %all-reduce.6.cloned.1.call-done = f32[1,264,256]{2,1,0:T(8,128)} async-done(((f32[1,264,256]{2,1,0:T(8,128)}), f32[1,264,256]{2,1,0:T(8,128)}) %all-reduce.6.cloned.1.call-update) | async-done | bytes 270352 | tf_op jit(solution)/shard_map/psum | solution.py:519
  130.0 0.0 all-gather.2.cloned.1.call-update
  130.0 1.9 copy-done.2
  131.9 39.2 %propagate.1.part_ref = f32[256,256]{1,0:T(8,128)S(1)} custom-call(f32[256,16,512]{2,1,0:T(8,128)} %basis_ref.3, f32[6,256,512]{2,1,0:T(8,128)S(1)} %copy-done.2, f32[5,20,512]{2,1,0:T(8,128)S(1)} %slice.80.fg_ref, f32[5,20,512]{2,1,0:T(8,128)S(1)} %slice.87.lg_ref), custom_call_target="tpu_custom_call" | custom-call | flops 41943040000 | bytes 8388608 | tf_op jit(solution)/shard_map/propagate/pallas_call | solution.py:536
  171.1 20.4 %spread.1.prop_ref = f32[4,256,256]{2,1,0:T(8,128)S(1)} custom-call(f32[256,256]{1,0:T(8,128)S(1)} %propagate.1.part_ref), custom_call_target="tpu_custom_call" | custom-call | tf_op jit(solution)/shard_map/spread/pallas_call | solution.py:554
  191.5 0.0 all-gather.2.cloned.1.call-done
  191.5 0.8 slice.89
  192.3 1.3 slice.88.info_ref
  193.6 25.7 %join.1 = f32[5,256]{1,0:T(8,128)S(1)} custom-call(f32[4,256,256]{2,1,0:T(8,128)S(1)} %spread.1.prop_ref, f32[4,256,256]{2,1,0:T(8,128)S(1)} %slice.88.info_ref, f32[4,256]{1,0:T(4,128)S(1)} %bitcast.52), custom_call_target="tpu_custom_call" | custom-call | tf_op jit(solution)/shard_map/join/pallas_call | solution.py:568
  219.3 0.6 dynamic-slice_bitcast_fusion
  219.9 4.6 %multiply_reduce_fusion = f32[16,512]{1,0:T(8,128)} fusion(f32[256,16,512]{2,1,0:T(8,128)} %basis_ref.3, f32[256]{0:T(256)S(1)} %bitcast.56), kind=kLoop, calls=%fused_computation | loop fusion | flops 4186112 | bytes 8422400 | tf_op jit(solution)/shard_map/reduce_sum | solution.py:580
  (28 shorter events, 0.3 us)
Async XLA Ops:
  7.2 122.8 %all-reduce.6.cloned.1.call-start = ((), (), s32[]{:S(2)}) async-start(), calls=%async_computation | async-start | bytes 540672 | tf_op jit(solution)/shard_map/psum | solution.py:519
  12.5 3.4 %copy-start = (f32[256,16,512]{2,1,0:T(8,128)S(1)}, f32[256,16,512]{2,1,0:T(8,128)}, u32[]{:S(2)}) copy-start(f32[256,16,512]{2,1,0:T(8,128)} %basis_ref.3) | copy-start | bytes 25165828
  40.4 1.6 copy-start.1
  43.0 148.5 %all-gather.2.cloned.1.call-start = ((), (), s32[]{:S(2)}) async-start(), calls=%async_computation.1 | async-start | bytes 1351680 | tf_op jit(solution)/shard_map/all_gather | solution.py:519
  130.0 1.9 copy-start.2
Sparse Core Ops, SparseCore 0:
  43.1 86.8 all-reduce.5
  131.6 16.1 all-gather.1

commit v3 on v2

--- a/solution.py
+++ b/solution.py
@@ -33,10 +33,10 @@
     )
 
 
-def dot3(a, b):
+def dot3(a, b, dims=NN):
     ah, al = split(a)
     bh, bl = split(b)
-    return dot16(ah, bh, NN) + dot16(ah, bl, NN) + dot16(al, bh, NN)
+    return dot16(ah, bh, dims) + dot16(ah, bl, dims) + dot16(al, bh, dims)
 
 
 MESH = pl.DeviceIdType.MESH
@@ -49,8 +49,8 @@
 
 
 def edge_kernel(
-    chips, tiles, basis_ref, cells_ref, counts_ref, weights_ref, halo_ref, fringe_ref, info_ref,
-    rhs_ref, edge, xh, xl, first_send, first_recv, cell_send, cell_recv, over_send, over_recv,
+    chips, tiles, basis_ref, d_ref, dx_ref, dy_ref, sea_ref, counts_ref, weights_ref, halo_ref, fringe_ref, info_ref,
+    edge, cells_ref, rhs_ref, xh, xl, first_send, first_recv, cell_send, cell_recv, over_send, over_recv,
     mate_send, mate_recv,
 ):
     width, rows, columns = basis_ref.shape
@@ -69,6 +69,13 @@
     for peer in ((tile + tiles - 1) % tiles, (tile + 1) % tiles):
         pl.semaphore_signal(barrier, inc=1, device_id={"tile": peer}, device_id_type=MESH)
 
+    cells_ref[...] = jnp.zeros_like(cells_ref)
+    for i, ref in enumerate((d_ref, dx_ref, dy_ref, sea_ref)):
+        for r in range(HALF):
+            cells_ref[r, i : i + 1, :] = ref[r : r + 1, :]
+            last = rows - HALF + r
+            cells_ref[HALF + r, i : i + 1, :] = ref[last : last + 1, :]
+
     def cut(j, _):
         x = basis_ref[pl.ds(mine + 8 * j, 8)]
         y = jnp.swapaxes(x, 0, 1)
@@ -85,7 +92,7 @@
 
     def send(side):
         other = 1 - side
-        first = 0 if side == 0 else rows - HALF
+        first = side * HALF
         return (
             remote(edge.at[pl.ds(side * HALF, HALF)], part(other, mine), first_send.at[side],
                    first_recv.at[other], tile=near[side]),
@@ -143,7 +150,7 @@
         x = a.astype(jnp.float32) + b.astype(jnp.float32)
         yh, yl = split(x * counts_ref[pl.ds(r, 1), :])
         z = x * weights_ref[pl.ds(r, 1), :]
-        info_ref[...] += dot16(a, yh, NT) + dot16(a, yl, NT) + dot16(b, yh, NT)
+        info_ref[:width, :] += dot16(a, yh, NT) + dot16(a, yl, NT) + dot16(b, yh, NT)
         part_sum = z[:, :128]
         for c in range(128, columns, 128):
             part_sum += z[:, c : c + 128]
@@ -182,9 +189,10 @@
             for copy in send(side):
                 copy.wait_send()
 
+    info_ref[width:, :] = dot32(jnp.ones((8, 128), jnp.float32), rhs_ref[...], NT)
+
 
 def spread_kernel(chips, tiles, part_ref, out_ref, land, s1, r1, s2, r2, s3, r3, s4, r4):
-    rows = part_ref.shape[0] // tiles
     group, tile = lax.axis_index("tm"), lax.axis_index("tile")
     chip, core = group // 2, group % 2
     mate = group + 1 - 2 * core
@@ -198,14 +206,11 @@
         pl.semaphore_signal(barrier, inc=1, device_id={"tile": peer}, device_id_type=MESH)
     pl.semaphore_wait(barrier, chips + tiles - 1)
 
-    def lines(t):
-        return pl.ds(pl.multiple_of(t * rows, rows), rows)
-
     def slot(g, t):
-        return out_ref.at[g, lines(t), :]
+        return out_ref.at[g, t]
 
     def scatter(d):
-        return remote(part_ref.at[lines(far[d]), :], land.at[d], s1.at[d], r1.at[d], tile=far[d])
+        return remote(part_ref.at[far[d]], land.at[d], s1.at[d], r1.at[d], tile=far[d])
 
     def gather(d):
         return remote(slot(group, tile), slot(group, tile), s2.at[d], r2.at[d], tile=far[d])
@@ -223,11 +228,11 @@
 
     for d in range(tiles - 1):
         scatter(d).start()
-    total = part_ref[lines(tile), :]
+    total = part_ref[tile]
     for d in range(tiles - 1):
         scatter(d).wait_recv()
         total = total + land[d]
-    out_ref[group, lines(tile), :] = total
+    out_ref[group, tile] = total
     for d in range(tiles - 1):
         gather(d).start()
     for d in range(tiles):
@@ -252,14 +257,42 @@
 
 
 def stencil_kernel(
-    rows, block, basis_ref, halo_ref, fg_ref, lg_ref, prop_ref, turned, gf, gl, f1, l1, f2, l2, fh, fl, lh, ll
+    tiles, block, basis_ref, d_ref, dx_ref, dy_ref, sea_ref, fringe_ref, halo_ref, info_ref, part_ref,
+    prop_ref, turned, gf, gl, f1, l1, f2, l2, fh, fl, lh, ll
 ):
-    width, _, columns = basis_ref.shape
+    width, rows, columns = basis_ref.shape
     halves = block // 8
-    for which, (src, dst) in enumerate(((fg_ref, gf), (lg_ref, gl))):
-        for i in range(5):
-            for r in range(src.shape[1]):
-                dst[i, r] = jnp.broadcast_to(src[i, r : r + 1, :], (8, columns))
+    column = lax.broadcasted_iota(jnp.int32, (8, columns), 1)
+
+    def cell(ref, i, r):
+        if r < 0:
+            line = fringe_ref[r + HALF, i : i + 1, :]
+        elif r >= rows:
+            line = fringe_ref[r - rows + HALF, i : i + 1, :]
+        else:
+            line = ref[r : r + 1, :]
+        return jnp.broadcast_to(line, (8, columns))
+
+    for r in range(-HALF, rows + HALF):
+        d, dx, dy, sea = (
+            cell(ref, i, r) for i, ref in enumerate((d_ref, dx_ref, dy_ref, sea_ref))
+        )
+        center = sea * (1.0 - 4.0 * d)
+        east = sea * (d * (1.0 - dx))
+        west = sea * (d * (1.0 + dx))
+        north = jnp.where(column == columns - 1, 0.0, sea * (d * (1.0 - dy)))
+        south = jnp.where(column == 0, 0.0, sea * (d * (1.0 + dy)))
+        at = r + HALF - 1
+        if 0 <= at < rows + 2 * (HALF - 1):
+            for i, gain in enumerate((center, east, west, north, south)):
+                gf[i, at] = gain
+            gl[0, at] = center
+            gl[3, at] = pltpu.roll(south, columns - 1, 1)
+            gl[4, at] = pltpu.roll(north, 1, 1)
+        if 0 <= at - 1 < rows + 2 * (HALF - 1):
+            gl[1, at - 1] = west
+        if 0 <= at + 1 < rows + 2 * (HALF - 1):
+            gl[2, at + 1] = east
 
     def rolled(x):
         return pltpu.roll(x, columns - 1, 1), pltpu.roll(x, 1, 1)
@@ -324,6 +357,11 @@
         return 0
 
     lax.fori_loop(0, rows, row, 0)
+    lines = width // tiles
+    for n in range(tiles):
+        part_ref[n, :lines, :] = prop_ref[n * lines : (n + 1) * lines, :]
+        part_ref[n, lines : 2 * lines, :] = info_ref[n * lines : (n + 1) * lines, :]
+        part_ref[n, 2 * lines :, :] = info_ref[width:, :]
 
 
 def eye_of(n):
@@ -344,7 +382,7 @@
         size = jnp.maximum(size, jnp.sum(r * r))
 
     def small(c):
-        return jnp.logical_not(c[1] <= 1e-4) & (c[0] < 30)
+        return jnp.logical_not(c[1] <= 1e-2) & (c[0] < 30)
 
     def grow(carry):
         it, _ = carry
@@ -362,7 +400,7 @@
     def residual():
         size = 0.0
         for a, x, t in zip(mats, invs, tmps):
-            r = eye - dot32(a[...], x[...])
+            r = eye - dot3(a[...], x[...])
             t[...] = r
             size = jnp.maximum(size, jnp.sum(r * r))
         return size
@@ -402,14 +440,15 @@
         x[...] += dot3(x[...], t[...])
 
 
-def join_kernel(groups, scale_prop, scale_obs, prop_ref, info_ref, rhs_ref, out_ref, s, x, t, w):
-    n = prop_ref.shape[1]
+def join_kernel(groups, scale_prop, scale_obs, sums_ref, out_ref, s, x, t, w):
+    n = sums_ref.shape[3]
+    lines = n // sums_ref.shape[1]
     middle = groups // 2
     q = q_inverse
     eye = eye_of(n)
 
     def prop(g):
-        return prop_ref[g] * scale_prop
+        return sums_ref[g, :, :lines, :].reshape(n, n) * scale_prop
 
     def diagonal(i):
         value = ridge * eye
@@ -417,7 +456,7 @@
             p = prop(i)
             value = value + q * dot32(p, p, TN)
         if i > 0:
-            value = value + (q * eye + info_ref[i - 1] * scale_obs)
+            value = value + (q * eye + sums_ref[i - 1, :, lines : 2 * lines, :].reshape(n, n) * scale_obs)
             if i < groups:
                 value = value + ridge * eye
         return value
@@ -425,7 +464,7 @@
     def right(i):
         if i == 0:
             return jnp.zeros((8, n), jnp.float32)
-        return jnp.broadcast_to(rhs_ref[i - 1 : i, :] * scale_obs, (8, n))
+        return sums_ref[i - 1, 0, 2 * lines :, :] * scale_obs
 
     for i in range(groups + 1):
         s[i] = diagonal(i)
@@ -438,12 +477,12 @@
         for i in todo:
             if i == top:
                 p = prop(i)
-                w[i] = q * dot32(x[i], p, NT)
+                w[i] = q * dot3(x[i], p, NT)
                 s[i + 1] -= q * dot32(p, w[i])
                 vec[i + 1] = vec[i + 1] + dot32(vec[i], w[i])
             else:
                 p = prop(i - 1)
-                w[i] = q * dot32(x[i], p)
+                w[i] = q * dot3(x[i], p)
                 s[i - 1] -= q * dot32(p, w[i], TN)
                 vec[i - 1] = vec[i - 1] + dot32(vec[i], w[i])
     invert([s.at[middle]], [x.at[middle]], [t.at[middle]])
@@ -459,13 +498,6 @@
 VMEM = pltpu.VMEM
 
 
-def moved(x, by, dim):
-    zero = jnp.zeros_like(lax.slice_in_dim(x, 0, 1, axis=dim))
-    if by > 0:
-        return jnp.concatenate([lax.slice_in_dim(x, 1, x.shape[dim], axis=dim), zero], axis=dim)
-    return jnp.concatenate([zero, lax.slice_in_dim(x, 0, x.shape[dim] - 1, axis=dim)], axis=dim)
-
-
 def shards(basis, diffusion, drift_x, drift_y, land_sea, obs_cells, obs_values):
     width, rows, columns = basis.shape
     nobs = obs_cells.shape[1]
@@ -474,10 +506,7 @@
     group = lax.axis_index("tm")
 
     chips = groups // 2
-    zeros = jnp.zeros_like(diffusion[0])
-    cells = jnp.stack(
-        [diffusion[0], drift_x[0], drift_y[0], land_sea.astype(jnp.float32)] + [zeros] * 4, axis=1
-    )
+    cells = (diffusion[0], drift_x[0], drift_y[0], land_sea.astype(jnp.float32))
     offset = lax.axis_index("tile") * (rows * columns)
     local = obs_cells[0] - offset
     inside = (local >= 0) & (local < rows * columns)
@@ -495,17 +524,18 @@
     share = width // groups
     DMA = pltpu.SemaphoreType.DMA
     whole = pl.BlockSpec(memory_space=VMEM)
-    halo, fringe, info, rhs = pl.pallas_call(
+    halo, fringe, info = pl.pallas_call(
         functools.partial(edge_kernel, chips, tiles),
         out_shape=(
             jax.ShapeDtypeStruct((2 * HALF, width, columns), jnp.float32),
             jax.ShapeDtypeStruct((2 * HALF, 8, columns), jnp.float32),
-            jax.ShapeDtypeStruct((width, width), jnp.float32),
-            jax.ShapeDtypeStruct((width, 128), jnp.float32),
+            jax.ShapeDtypeStruct((width + 8, width), jnp.float32),
         ),
-        in_specs=[whole] * 4,
-        out_specs=[whole] * 4,
+        in_specs=[whole] * 7,
+        out_specs=[whole] * 3,
         scratch_shapes=[VMEM((2 * HALF, share, columns), jnp.float32)]
+        + [VMEM((2 * HALF, 8, columns), jnp.float32)]
+        + [VMEM((width, 128), jnp.float32)]
         + [VMEM((rows, width, columns), jnp.bfloat16)] * 2
         + [DMA((2,))] * 4
         + [DMA((2, max(chips - 1, 1)))] * 2
@@ -514,31 +544,17 @@
             vmem_limit_bytes=40 << 20, collective_id=0, has_side_effects=True
         ),
         name="edges",
-    )(basis, cells, hits[:rows], hits[rows:])
-    info = jnp.concatenate([info, jnp.broadcast_to(jnp.sum(rhs, axis=1)[None, :], (8, width))])
-    info = lax.all_gather(lax.psum(info, "tile"), "tm", axis=0)
-
-    cells = jnp.concatenate([fringe[:HALF], cells, fringe[HALF:]], axis=0)
-    d, dx, dy, sea = cells[:, 0], cells[:, 1], cells[:, 2], cells[:, 3]
-    column = lax.broadcasted_iota(jnp.int32, d.shape, 1)
-    center = sea * (1.0 - 4.0 * d)
-    east = sea * (d * (1.0 - dx))
-    west = sea * (d * (1.0 + dx))
-    north = jnp.where(column == columns - 1, 0.0, sea * (d * (1.0 - dy)))
-    south = jnp.where(column == 0, 0.0, sea * (d * (1.0 + dy)))
-    forward = jnp.stack([center, east, west, north, south])[:, 1:-1]
-    backward = jnp.stack(
-        [center, moved(west, 1, 0), moved(east, -1, 0), moved(south, 1, 1), moved(north, -1, 1)]
-    )[:, 1:-1]
-
+    )(basis, *cells, hits[:rows], hits[rows:])
     block = 16
     edge_rows = rows + 2 * (HALF - 1)
-    prop = pl.pallas_call(
-        functools.partial(stencil_kernel, rows, block),
-        out_shape=jax.ShapeDtypeStruct((width, width), jnp.float32),
-        in_specs=[pl.BlockSpec(memory_space=VMEM)] * 4,
+    lines = 2 * width // tiles + 8
+    part = pl.pallas_call(
+        functools.partial(stencil_kernel, tiles, block),
+        out_shape=jax.ShapeDtypeStruct((tiles, lines, width), jnp.float32),
+        in_specs=[whole] * 8,
         out_specs=pl.BlockSpec(memory_space=VMEM),
-        scratch_shapes=[VMEM((rows, block // 8, 8, columns), jnp.float32)]
+        scratch_shapes=[VMEM((width, width), jnp.float32)]
+        + [VMEM((rows, block // 8, 8, columns), jnp.float32)]
         + [VMEM((5, edge_rows, 8, columns), jnp.float32)] * 2
         + [VMEM((edge_rows, block // 8, 8, columns), jnp.float32)] * 4
         + [VMEM((rows, width, columns), jnp.bfloat16)] * 4,
@@ -549,14 +565,14 @@
             transcendentals=0,
         ),
         name="propagate",
-    )(basis, halo, forward, backward)
-
-    props = pl.pallas_call(
+    )(basis, *cells, fringe, halo, info)
+
+    sums = pl.pallas_call(
         functools.partial(spread_kernel, chips, tiles),
-        out_shape=jax.ShapeDtypeStruct((groups, width, width), jnp.float32),
+        out_shape=jax.ShapeDtypeStruct((groups, tiles, lines, width), jnp.float32),
         in_specs=[whole],
         out_specs=whole,
-        scratch_shapes=[VMEM((tiles - 1, width // tiles, width), jnp.float32)]
+        scratch_shapes=[VMEM((tiles - 1, lines, width), jnp.float32)]
         + [DMA((tiles - 1,))] * 4
         + [DMA((tiles, max(chips - 1, 1)))] * 2
         + [DMA((tiles, chips))] * 2,
@@ -564,18 +580,18 @@
             vmem_limit_bytes=16 << 20, collective_id=1, has_side_effects=True
         ),
         name="spread",
-    )(prop)
+    )(part)
     states = pl.pallas_call(
         functools.partial(
             join_kernel, groups, 1.0 / (rows * columns * tiles), 1.0 / nobs
         ),
         out_shape=jax.ShapeDtypeStruct((groups + 1, width), jnp.float32),
-        in_specs=[pl.BlockSpec(memory_space=VMEM)] * 3,
-        out_specs=pl.BlockSpec(memory_space=VMEM),
+        in_specs=[whole],
+        out_specs=whole,
         scratch_shapes=[VMEM((groups + 1, width, width), jnp.float32)] * 4,
         compiler_params=pltpu.CompilerParams(vmem_limit_bytes=48 << 20),
         name="join",
-    )(props, info[:, :width], info[:, width])
+    )(sums)
     coeffs = lax.dynamic_slice_in_dim(states, group, 2, axis=0)
     end_fields = jnp.sum(coeffs[1][:, None, None] * basis, axis=0)
     return coeffs[None], end_fields[None]

time: 232 us -> 157 us (0.68)
  waiting for transfers between devices: 86.3 us -> 0 us
  Pallas kernels: 110 us -> 141 us
  between operations: 14.3 us -> 0.73 us
  local copies, waits for them, and re-layouts: 12.4 us -> 6.28 us
    psum x1 -> x0, waiting for transfers between devices: 86.2 us -> none  [shards(): info = lax.all_gather(lax.psum(info, 'tile'), 'tm', axis=0)]
    pallas_call x1, Pallas kernels: 20.4 us -> 55 us  [shards(): pl.pallas_call(functools.partial(spread_kernel, chips, tiles), out_shape=...]
    pallas_call x1, Pallas kernels: 25.7 us -> 22 us  [shards(): pl.pallas_call(functools.partial(join_kernel, groups, 1.0 / (rows * colum...]
    unnamed x14, local copies, waits for them, and re-layouts: 9.23 us -> 5.67 us
  transfers between devices with their start and end apart: 2 -> 0, of which waited for: 1 -> 0; matrix products, arithmetic and copies ran while one was open for 0% -> 0% of each run, Pallas kernels for 26% -> 0%
where the time goes in v3:
time: 157 us; the launch traced here: 156 us
  Pallas kernels  141 us (90%)
  other arithmetic  6.8 us (4%)
  local copies, waits for them, and re-layouts  6.28 us (4%)
    pallas_call x1, Pallas kernels, shards(): pl.pallas_call(functools.partial(spread_kernel, chips, tiles), out_shape=...  55 us
    pallas_call x1, Pallas kernels, shards(): pl.pallas_call(functools.partial(stencil_kernel, tiles, block), out_shape...  39.3 us
    pallas_call x1, Pallas kernels, shards(): pl.pallas_call(functools.partial(edge_kernel, chips, tiles), out_shape=(j...  24.8 us
    pallas_call x1, Pallas kernels, shards(): pl.pallas_call(functools.partial(join_kernel, groups, 1.0 / (rows * colum...  22 us
    unnamed x14, local copies, waits for them, and re-layouts  5.67 us
    reduce_sum x1, other arithmetic, shards(): end_fields = jnp.sum(coeffs[1][:, None, None] * basis, axis=0)  4.62 us

profile of v3, /device:TPU:0, one launch (start us, length us, event | category | flops | bytes accessed | tf_op | source)
XLA Modules:
  0.0 155.6 jit_solution(7888390083016615092)
XLA Ops:
  0.6 0.0 copy-start.2
  0.6 0.0 copy-start.4
  0.7 0.0 copy-start.6
  0.7 0.7 and_select_fusion.2
  1.4 0.7 fusion.5
  2.1 0.6 fusion
  2.7 0.8 convert_element_type.7.sea_ref
  3.5 0.0 copy-start
  3.5 3.4 %copy-done = f32[256,16,512]{2,1,0:T(8,128)S(1)} copy-done((f32[256,16,512]{2,1,0:T(8,128)S(1)}, f32[256,16,512]{2,1,0:T(8,128)}, u32[]{:S(2)}) %copy-start) | copy-done | bytes 8388632
  6.9 0.0 copy-start.1
  6.9 0.8 copy-done.1
  7.6 0.0 copy-start.3
  7.6 0.8 copy-done.3
  8.4 0.0 copy-start.5
  8.4 0.8 copy-done.5
  9.1 24.8 %edges.1 = (f32[6,256,512]{2,1,0:T(8,128)S(1)}, f32[6,8,512]{2,1,0:T(8,128)S(1)}, f32[264,256]{1,0:T(8,128)S(1)}) custom-call(f32[256,16,512]{2,1,0:T(8,128)S(1)} %copy-done, f32[16,512]{1,0:T(8,128)S(1)} %bitcast.10, f32[16,512]{1,0:T(8,128)S(1)} %bitcast.12, f32[16,512]{1,0:T(8,128)S(1)} %bitcast.14, f32[16,512]{1,0:T(8,128)S(1)} %convert_element_type.7.sea_ref, ...), custom_call_target="tpu_custom_call" | custom-call | tf_op jit(solution)/shard_map/edges/pallas_call | solution.py:527
  33.9 0.0 copy-done.2
  33.9 0.0 copy-done.4
  34.0 0.0 copy-done.6
  34.0 39.3 %propagate.1.part_ref = f32[8,72,256]{2,1,0:T(8,128)S(1)} custom-call(f32[256,16,512]{2,1,0:T(8,128)} %basis_ref.3, f32[16,512]{1,0:T(8,128)S(1)} %bitcast.11, f32[16,512]{1,0:T(8,128)S(1)} %bitcast.13, f32[16,512]{1,0:T(8,128)S(1)} %bitcast.15, f32[16,512]{1,0:T(8,128)S(1)} %convert_element_type.7.sea_ref, f32[6,8,512]{2,1,0:T(8,128)S(1)} %get-tuple-element.5.fringe_ref, ...), custom_call_target="tpu_custom_call" | custom-call | flops 41943040000 | bytes 8388608 | tf_op jit(solution)/shard_map/propagate/pallas_call | solution.py:551
  73.3 55.0 %spread.1.sums_ref = f32[4,8,72,256]{3,2,1,0:T(8,128)S(1)} custom-call(f32[8,72,256]{2,1,0:T(8,128)S(1)} %propagate.1.part_ref), custom_call_target="tpu_custom_call" | custom-call | tf_op jit(solution)/shard_map/spread/pallas_call | solution.py:570
  128.3 22.0 %join.1 = f32[5,256]{1,0:T(8,128)S(1)} custom-call(f32[4,8,72,256]{3,2,1,0:T(8,128)S(1)} %spread.1.sums_ref), custom_call_target="tpu_custom_call" | custom-call | tf_op jit(solution)/shard_map/join/pallas_call | solution.py:584
  150.3 4.6 %multiply_reduce_fusion = f32[16,512]{1,0:T(8,128)} fusion(f32[256,16,512]{2,1,0:T(8,128)} %basis_ref.3, f32[256]{0:T(256)S(1)} %bitcast.19), kind=kLoop, calls=%fused_computation | loop fusion | flops 4186112 | bytes 8422400 | tf_op jit(solution)/shard_map/reduce_sum | solution.py:596
  155.0 0.6 dynamic-slice_bitcast_fusion
  (4 shorter events, 0.0 us)
Async XLA Ops:
  0.6 33.3 %copy-start.2 = (f32[1,16,512]{2,1,0:T(8,128)S(1)}, f32[1,16,512]{2,1,0:T(8,128)}, u32[]{:S(2)}) copy-start(f32[1,16,512]{2,1,0:T(8,128)} %param.8) | copy-start | bytes 98308
  0.6 33.3 %copy-start.4 = (f32[1,16,512]{2,1,0:T(8,128)S(1)}, f32[1,16,512]{2,1,0:T(8,128)}, u32[]{:S(2)}) copy-start(f32[1,16,512]{2,1,0:T(8,128)} %param.9) | copy-start | bytes 98308
  0.7 33.3 %copy-start.6 = (f32[1,16,512]{2,1,0:T(8,128)S(1)}, f32[1,16,512]{2,1,0:T(8,128)}, u32[]{:S(2)}) copy-start(f32[1,16,512]{2,1,0:T(8,128)} %param.10) | copy-start | bytes 98308
  3.5 3.4 %copy-start = (f32[256,16,512]{2,1,0:T(8,128)S(1)}, f32[256,16,512]{2,1,0:T(8,128)}, u32[]{:S(2)}) copy-start(f32[256,16,512]{2,1,0:T(8,128)} %basis_ref.3) | copy-start | bytes 25165828
  6.9 0.8 copy-start.1
  7.6 0.8 copy-start.3
  8.4 0.8 copy-start.5

commit v4 on v3

--- a/solution.py
+++ b/solution.py
@@ -9,6 +9,7 @@
 
 STEPS = 6
 HALF = STEPS // 2
+CHUNKS = 4
 
 q_inverse = 10.0
 ridge = 0.1
@@ -49,8 +50,8 @@
 
 
 def edge_kernel(
-    chips, tiles, basis_ref, d_ref, dx_ref, dy_ref, sea_ref, counts_ref, weights_ref, halo_ref, fringe_ref, info_ref,
-    edge, cells_ref, rhs_ref, xh, xl, first_send, first_recv, cell_send, cell_recv, over_send, over_recv,
+    chips, tiles, basis_ref, d_ref, dx_ref, dy_ref, sea_ref, where_ref, value_ref, halo_ref, fringe_ref, info_ref,
+    edge, cells_ref, hits_ref, rhs_ref, xh, xl, first_send, first_recv, cell_send, cell_recv, over_send, over_recv,
     mate_send, mate_recv,
 ):
     width, rows, columns = basis_ref.shape
@@ -58,6 +59,7 @@
     chip, core = group // 2, group % 2
     mate = group + 1 - 2 * core
     share = edge.shape[1]
+    piece = share // CHUNKS
     mine = pl.multiple_of(group * share, share)
     others = [((chip + i) % chips) * 2 + core for i in range(1, chips)]
     has = (tile > 0, tile < tiles - 1)
@@ -72,9 +74,9 @@
     cells_ref[...] = jnp.zeros_like(cells_ref)
     for i, ref in enumerate((d_ref, dx_ref, dy_ref, sea_ref)):
         for r in range(HALF):
-            cells_ref[r, i : i + 1, :] = ref[r : r + 1, :]
+            cells_ref[r, i : i + 1, :] = ref[r : r + 1, :].astype(jnp.float32)
             last = rows - HALF + r
-            cells_ref[HALF + r, i : i + 1, :] = ref[last : last + 1, :]
+            cells_ref[HALF + r, i : i + 1, :] = ref[last : last + 1, :].astype(jnp.float32)
 
     def cut(j, _):
         x = basis_ref[pl.ds(mine + 8 * j, 8)]
@@ -87,42 +89,54 @@
     lax.fori_loop(0, share // 8, cut, 0)
     pl.semaphore_wait(barrier, chips + 2)
 
-    def part(side, k):
-        return halo_ref.at[pl.ds(side * HALF, HALF), pl.ds(pl.multiple_of(k, share), share), :]
-
-    def send(side):
+    def part(side, g, j):
+        k = pl.multiple_of(g * share + j * piece, piece)
+        return halo_ref.at[pl.ds(side * HALF, HALF), pl.ds(k, piece), :]
+
+    def ours(side, j):
+        return edge.at[pl.ds(side * HALF, HALF), pl.ds(j * piece, piece), :]
+
+    def send(side, j):
         other = 1 - side
-        first = side * HALF
-        return (
-            remote(edge.at[pl.ds(side * HALF, HALF)], part(other, mine), first_send.at[side],
-                   first_recv.at[other], tile=near[side]),
-            remote(cells_ref.at[pl.ds(first, HALF)], fringe_ref.at[pl.ds(other * HALF, HALF)],
-                   cell_send.at[side], cell_recv.at[other], tile=near[side]),
-        )
-
-    def arrival(side):
-        return (
-            remote(edge.at[pl.ds(side * HALF, HALF)], part(side, mine), first_send.at[side],
-                   first_recv.at[side], tile=near[side]),
-            remote(cells_ref.at[pl.ds(0, HALF)], fringe_ref.at[pl.ds(side * HALF, HALF)],
-                   cell_send.at[side], cell_recv.at[side], tile=near[side]),
-        )
-
-    def over(side, i):
-        return remote(part(side, mine), part(side, mine), over_send.at[side, i],
-                      over_recv.at[side, i], tm=others[i])
-
-    def to_mate(side, i):
-        k = (((chip - i + chips) % chips) * 2 + core) * share
-        return remote(part(side, k), part(side, k), mate_send.at[side, i], mate_recv.at[side, i],
-                      tm=mate)
+        return remote(ours(side, j), part(other, group, j), first_send.at[side, j],
+                      first_recv.at[other, j], tile=near[side])
+
+    def arrival(side, j):
+        return remote(ours(side, j), part(side, group, j), first_send.at[side, j],
+                      first_recv.at[side, j], tile=near[side])
+
+    def send_cells(side):
+        other = 1 - side
+        return remote(cells_ref.at[pl.ds(side * HALF, HALF)],
+                      fringe_ref.at[pl.ds(other * HALF, HALF)],
+                      cell_send.at[side], cell_recv.at[other], tile=near[side])
+
+    def cells_arrival(side):
+        return remote(cells_ref.at[pl.ds(side * HALF, HALF)],
+                      fringe_ref.at[pl.ds(side * HALF, HALF)],
+                      cell_send.at[side], cell_recv.at[side], tile=near[side])
+
+    def over(side, j, i):
+        place = part(side, group, j)
+        return remote(place, place, over_send.at[side, j, i], over_recv.at[side, j, i],
+                      tm=others[i])
+
+    def to_mate(side, j, i):
+        place = part(side, ((chip - i + chips) % chips) * 2 + core, j)
+        return remote(place, place, mate_send.at[side, j, i], mate_recv.at[side, j, i], tm=mate)
+
+    for j in range(CHUNKS):
+        for side in range(2):
+
+            @pl.when(has[side])
+            def _():
+                send(side, j).start()
 
     for side in range(2):
 
         @pl.when(has[side])
         def _():
-            for copy in send(side):
-                copy.start()
+            send_cells(side).start()
 
         @pl.when(jnp.logical_not(has[side]))
         def _():
@@ -133,6 +147,15 @@
                 (HALF,) + fringe_ref.shape[1:], jnp.float32
             )
 
+    nobs = where_ref.shape[1]
+    local = where_ref[...] - tile * (rows * columns)
+    first = lax.broadcasted_iota(jnp.int32, (rows, nobs), 0) * columns
+    in_row = (local >= first) & (local < first + columns)
+    col_of = local - jnp.sum(jnp.where(in_row, first, 0), axis=0, keepdims=True)
+    in_col = (lax.broadcasted_iota(jnp.int32, (columns, nobs), 0) == col_of).astype(jnp.float32)
+    hits_ref[:rows, :] = dot32(in_row.astype(jnp.float32), in_col, NT)
+    hits_ref[rows:, :] = dot32(jnp.where(in_row, value_ref[...], 0.0), in_col, NT)
+
     def turn(j, _):
         k = pl.multiple_of(16 * j, 16)
         y = jnp.swapaxes(basis_ref[pl.ds(k, 16)], 0, 1)
@@ -148,8 +171,8 @@
     def row(r, _):
         a, b = xh[r], xl[r]
         x = a.astype(jnp.float32) + b.astype(jnp.float32)
-        yh, yl = split(x * counts_ref[pl.ds(r, 1), :])
-        z = x * weights_ref[pl.ds(r, 1), :]
+        yh, yl = split(x * hits_ref[pl.ds(r, 1), :])
+        z = x * hits_ref[pl.ds(rows + r, 1), :]
         info_ref[:width, :] += dot16(a, yh, NT) + dot16(a, yl, NT) + dot16(b, yh, NT)
         part_sum = z[:, :128]
         for c in range(128, columns, 128):
@@ -157,37 +180,42 @@
         rhs_ref[...] += part_sum
         return 0
 
-    lax.fori_loop(0, rows // 2, row, 0)
-    for side in range(2):
-
-        @pl.when(has[side])
-        def _():
-            arrival(side)[0].wait_recv()
-            for i in range(chips - 1):
-                over(side, i).start()
-            to_mate(side, 0).start()
-
-    lax.fori_loop(rows // 2, rows, row, 0)
+    for j in range(CHUNKS):
+        lax.fori_loop(j * rows // CHUNKS, (j + 1) * rows // CHUNKS, row, 0)
+        for side in range(2):
+
+            @pl.when(has[side])
+            def _():
+                arrival(side, j).wait_recv()
+                for i in range(chips - 1):
+                    over(side, j, i).start()
+                to_mate(side, j, 0).start()
+                if j:
+                    for i in range(chips - 1):
+                        over(side, j - 1, i).wait_recv()
+                        to_mate(side, j - 1, i + 1).start()
+
     for side in range(2):
 
         @pl.when(has[side])
         def _():
             for i in range(chips - 1):
-                over(side, i).wait_recv()
-                to_mate(side, i + 1).start()
+                over(side, CHUNKS - 1, i).wait_recv()
+                to_mate(side, CHUNKS - 1, i + 1).start()
 
     for side in range(2):
 
         @pl.when(has[side])
         def _():
-            for i in range(chips):
-                to_mate(side, i).wait_recv()
-                to_mate(side, i).wait_send()
-            for i in range(chips - 1):
-                over(side, i).wait_send()
-            arrival(side)[1].wait_recv()
-            for copy in send(side):
-                copy.wait_send()
+            for j in range(CHUNKS):
+                for i in range(chips):
+                    to_mate(side, j, i).wait_recv()
+                    to_mate(side, j, i).wait_send()
+                for i in range(chips - 1):
+                    over(side, j, i).wait_send()
+                send(side, j).wait_send()
+            cells_arrival(side).wait_recv()
+            send_cells(side).wait_send()
 
     info_ref[width:, :] = dot32(jnp.ones((8, 128), jnp.float32), rhs_ref[...], NT)
 
@@ -271,7 +299,7 @@
             line = fringe_ref[r - rows + HALF, i : i + 1, :]
         else:
             line = ref[r : r + 1, :]
-        return jnp.broadcast_to(line, (8, columns))
+        return jnp.broadcast_to(line.astype(jnp.float32), (8, columns))
 
     for r in range(-HALF, rows + HALF):
         d, dx, dy, sea = (
@@ -440,7 +468,9 @@
         x[...] += dot3(x[...], t[...])
 
 
-def join_kernel(groups, scale_prop, scale_obs, sums_ref, out_ref, s, x, t, w):
+def join_kernel(
+    groups, scale_prop, scale_obs, sums_ref, basis_ref, coeff_ref, field_ref, s, x, t, w, st, col
+):
     n = sums_ref.shape[3]
     lines = n // sums_ref.shape[1]
     middle = groups // 2
@@ -492,7 +522,21 @@
     for i in range(middle + 1, groups + 1):
         state[i] = dot32(vec[i], x[i]) + dot32(state[i - 1], w[i], NT)
     for i in range(groups + 1):
-        out_ref[i : i + 1, :] = state[i][:1]
+        st[i] = state[i]
+    group = lax.axis_index("tm")
+    coeff_ref[0:1, :] = st[group][:1]
+    end = st[group + 1]
+    coeff_ref[1:2, :] = end[:1]
+    col[...] = dot32(eye, end, NT)
+
+    def add(j, total):
+        k = pl.multiple_of(8 * j, 8)
+        weights = col[pl.ds(k, 8), :]
+        for i in range(8):
+            total = total + weights[i : i + 1, 0:1] * basis_ref[k + i]
+        return total
+
+    field_ref[...] = lax.fori_loop(0, n // 8, add, jnp.zeros(field_ref.shape, jnp.float32))
 
 
 VMEM = pltpu.VMEM
@@ -503,24 +547,8 @@
     nobs = obs_cells.shape[1]
     groups = lax.axis_size("tm")
     tiles = lax.axis_size("tile")
-    group = lax.axis_index("tm")
-
     chips = groups // 2
-    cells = (diffusion[0], drift_x[0], drift_y[0], land_sea.astype(jnp.float32))
-    offset = lax.axis_index("tile") * (rows * columns)
-    local = obs_cells[0] - offset
-    inside = (local >= 0) & (local < rows * columns)
-    row_of = jnp.where(inside, local // columns, -1)
-    col_of = local % columns
-    in_row = lax.broadcasted_iota(jnp.int32, (rows, nobs), 0) == row_of[None, :]
-    in_col = (lax.broadcasted_iota(jnp.int32, (columns, nobs), 0) == col_of[None, :]).astype(
-        jnp.float32
-    )
-    hits = jnp.concatenate(
-        [in_row.astype(jnp.float32), jnp.where(in_row, obs_values[0][None, :], 0.0)], axis=0
-    )
-    hits = dot32(hits, in_col, NT)
-
+    cells = (diffusion[0], drift_x[0], drift_y[0], land_sea)
     share = width // groups
     DMA = pltpu.SemaphoreType.DMA
     whole = pl.BlockSpec(memory_space=VMEM)
@@ -535,16 +563,18 @@
         out_specs=[whole] * 3,
         scratch_shapes=[VMEM((2 * HALF, share, columns), jnp.float32)]
         + [VMEM((2 * HALF, 8, columns), jnp.float32)]
+        + [VMEM((2 * rows, columns), jnp.float32)]
         + [VMEM((width, 128), jnp.float32)]
         + [VMEM((rows, width, columns), jnp.bfloat16)] * 2
-        + [DMA((2,))] * 4
-        + [DMA((2, max(chips - 1, 1)))] * 2
-        + [DMA((2, chips))] * 2,
+        + [DMA((2, CHUNKS))] * 2
+        + [DMA((2,))] * 2
+        + [DMA((2, CHUNKS, max(chips - 1, 1)))] * 2
+        + [DMA((2, CHUNKS, chips))] * 2,
         compiler_params=pltpu.CompilerParams(
             vmem_limit_bytes=40 << 20, collective_id=0, has_side_effects=True
         ),
         name="edges",
-    )(basis, *cells, hits[:rows], hits[rows:])
+    )(basis, *cells, obs_cells, obs_values)
     block = 16
     edge_rows = rows + 2 * (HALF - 1)
     lines = 2 * width // tiles + 8
@@ -581,19 +611,21 @@
         ),
         name="spread",
     )(part)
-    states = pl.pallas_call(
+    coeffs, end_fields = pl.pallas_call(
         functools.partial(
             join_kernel, groups, 1.0 / (rows * columns * tiles), 1.0 / nobs
         ),
-        out_shape=jax.ShapeDtypeStruct((groups + 1, width), jnp.float32),
-        in_specs=[whole],
-        out_specs=whole,
-        scratch_shapes=[VMEM((groups + 1, width, width), jnp.float32)] * 4,
-        compiler_params=pltpu.CompilerParams(vmem_limit_bytes=48 << 20),
+        out_shape=(
+            jax.ShapeDtypeStruct((2, width), jnp.float32),
+            jax.ShapeDtypeStruct((rows, columns), jnp.float32),
+        ),
+        in_specs=[whole] * 2,
+        out_specs=[whole] * 2,
+        scratch_shapes=[VMEM((groups + 1, width, width), jnp.float32)] * 4
+        + [VMEM((groups + 1, 8, width), jnp.float32), VMEM((width, 8), jnp.float32)],
+        compiler_params=pltpu.CompilerParams(vmem_limit_bytes=40 << 20),
         name="join",
-    )(sums)
-    coeffs = lax.dynamic_slice_in_dim(states, group, 2, axis=0)
-    end_fields = jnp.sum(coeffs[1][:, None, None] * basis, axis=0)
+    )(sums, basis)
     return coeffs[None], end_fields[None]
 
 

time: 157 us -> 149 us (0.949)
  other arithmetic: 6.8 us -> 0.01 us
  Pallas kernels: 141 us -> 139 us
    pallas_call x1, Pallas kernels: 55 us -> 48.1 us  [shards(): pl.pallas_call(functools.partial(spread_kernel, chips, tiles), out_shape=...]
    reduce_sum x1 -> x0, other arithmetic: 4.62 us -> none  [shards(): end_fields = jnp.sum(coeffs[1][:, None, None] * basis, axis=0)]
    pallas_call x1, Pallas kernels: 22 us -> 25.4 us  [shards(): pl.pallas_call(functools.partial(join_kernel, groups, 1.0 / (rows * colum...]
    unnamed x14 -> x18, local copies, waits for them, and re-layouts: 5.67 us -> 7.78 us
where the time goes in v4:
time: 149 us; the launch traced here: 148 us
  Pallas kernels  139 us (93%)
  local copies, waits for them, and re-layouts  7.78 us (5%)
    pallas_call x1, Pallas kernels, shards(): pl.pallas_call(functools.partial(spread_kernel, chips, tiles), out_shape=...  48.1 us
    pallas_call x1, Pallas kernels, shards(): pl.pallas_call(functools.partial(stencil_kernel, tiles, block), out_shape...  39.9 us
    pallas_call x1, Pallas kernels, shards(): pl.pallas_call(functools.partial(edge_kernel, chips, tiles), out_shape=(j...  25.8 us
    pallas_call x1, Pallas kernels, shards(): pl.pallas_call(functools.partial(join_kernel, groups, 1.0 / (rows * colum...  25.4 us
    unnamed x18, local copies, waits for them, and re-layouts  7.78 us

profile of v4, /device:TPU:0, one launch (start us, length us, event | category | flops | bytes accessed | tf_op | source)
XLA Modules:
  0.0 147.6 jit_solution(4151029667501798838)
XLA Ops:
  0.6 0.0 copy-start
  0.6 3.4 %copy-done = f32[256,16,512]{2,1,0:T(8,128)S(1)} copy-done((f32[256,16,512]{2,1,0:T(8,128)S(1)}, f32[256,16,512]{2,1,0:T(8,128)}, u32[]{:S(2)}) %copy-start) | copy-done | bytes 8388632
  4.0 0.0 copy-start.1
  4.0 0.8 copy-done.1
  4.8 0.0 copy-start.2
  4.8 0.8 copy-done.2
  5.5 0.0 copy-start.3
  5.5 0.8 copy-done.3
  6.3 0.0 copy-start.4
  6.3 0.8 copy-done.4
  7.1 0.0 copy-start.5
  7.1 0.7 copy-done.5
  7.7 0.0 copy-start.6
  7.7 0.7 copy-done.6
  8.4 0.0 slice-start
  8.4 25.8 %edges.1 = (f32[6,256,512]{2,1,0:T(8,128)S(1)}, f32[6,8,512]{2,1,0:T(8,128)S(1)}, f32[264,256]{1,0:T(8,128)S(1)}) custom-call(f32[256,16,512]{2,1,0:T(8,128)S(1)} %copy-done, f32[16,512]{1,0:T(8,128)S(1)} %bitcast.7, f32[16,512]{1,0:T(8,128)S(1)} %bitcast.9, f32[16,512]{1,0:T(8,128)S(1)} %bitcast.11, s32[16,512]{1,0:T(8,128)S(1)} %copy-done.4, ...), custom_call_target="tpu_custom_call" | custom-call | tf_op jit(solution)/shard_map/edges/pallas_call | solution.py:555
  34.2 0.0 slice-start.1
  34.3 39.9 %propagate.1.part_ref = f32[8,72,256]{2,1,0:T(8,128)S(1)} custom-call(f32[256,16,512]{2,1,0:T(8,128)} %basis_ref.5, f32[16,512]{1,0:T(8,128)S(1)} %bitcast.8, f32[16,512]{1,0:T(8,128)S(1)} %bitcast.10, f32[16,512]{1,0:T(8,128)S(1)} %bitcast.12, s32[16,512]{1,0:T(8,128)S(1)} %copy-done.4, f32[6,8,512]{2,1,0:T(8,128)S(1)} %get-tuple-element.7.fringe_ref, ...), custom_call_target="tpu_custom_call" | custom-call | flops 41943040000 | bytes 8388608 | tf_op jit(solution)/shard_map/propagate/pallas_call | solution.py:581
  74.1 48.1 %spread.1.sums_ref = f32[4,8,72,256]{3,2,1,0:T(8,128)S(1)} custom-call(f32[8,72,256]{2,1,0:T(8,128)S(1)} %propagate.1.part_ref), custom_call_target="tpu_custom_call" | custom-call | tf_op jit(solution)/shard_map/spread/pallas_call | solution.py:600
  122.2 0.0 slice-done
  122.2 0.0 slice-done.1
  122.2 25.4 %join.1 = (f32[2,256]{1,0:T(2,128)}, f32[16,512]{1,0:T(8,128)}) custom-call(f32[4,8,72,256]{3,2,1,0:T(8,128)S(1)} %spread.1.sums_ref, f32[256,16,512]{2,1,0:T(8,128)S(1)} %bitcast.6), custom_call_target="tpu_custom_call" | custom-call | tf_op jit(solution)/shard_map/join/pallas_call | solution.py:614
  (1 shorter events, 0.0 us)
Async XLA Ops:
  0.6 3.4 %copy-start = (f32[256,16,512]{2,1,0:T(8,128)S(1)}, f32[256,16,512]{2,1,0:T(8,128)}, u32[]{:S(2)}) copy-start(f32[256,16,512]{2,1,0:T(8,128)} %basis_ref.5) | copy-start | bytes 25165828
  4.0 0.8 copy-start.1
  4.8 0.8 copy-start.2
  5.5 0.8 copy-start.3
  6.3 0.8 copy-start.4
  7.1 0.7 copy-start.5
  7.7 0.7 copy-start.6
  8.4 113.8 %slice-start = ((s8[8388608]{0:T(1024)(128)(4,1)}), s8[4194304]{0:T(1024)(128)(4,1)S(1)}, s32[]{:S(2)}) async-start(s8[8388608]{0:T(1024)(128)(4,1)} %bitcast.5), calls=%async_computation | async-start | bytes 8388608
  34.2 88.0 %slice-start.1 = ((s8[8388608]{0:T(1024)(128)(4,1)}), s8[4194304]{0:T(1024)(128)(4,1)S(1)}, s32[]{:S(2)}) async-start(s8[8388608]{0:T(1024)(128)(4,1)} %bitcast.5), calls=%async_computation.1 | async-start | bytes 8388608

commit v5 on v4

--- a/solution.py
+++ b/solution.py
@@ -484,7 +484,7 @@
         value = ridge * eye
         if i < groups:
             p = prop(i)
-            value = value + q * dot32(p, p, TN)
+            value = value + q * dot3(p, p, TN)
         if i > 0:
             value = value + (q * eye + sums_ref[i - 1, :, lines : 2 * lines, :].reshape(n, n) * scale_obs)
             if i < groups:
@@ -508,12 +508,12 @@
             if i == top:
                 p = prop(i)
                 w[i] = q * dot3(x[i], p, NT)
-                s[i + 1] -= q * dot32(p, w[i])
+                s[i + 1] -= q * dot3(p, w[i])
                 vec[i + 1] = vec[i + 1] + dot32(vec[i], w[i])
             else:
                 p = prop(i - 1)
                 w[i] = q * dot3(x[i], p)
-                s[i - 1] -= q * dot32(p, w[i], TN)
+                s[i - 1] -= q * dot3(p, w[i], TN)
                 vec[i - 1] = vec[i - 1] + dot32(vec[i], w[i])
     invert([s.at[middle]], [x.at[middle]], [t.at[middle]])
     state = {middle: dot32(vec[middle], x[middle])}

time: 149 us -> 149 us (level)
  no operation moved by 1% of the time
where the time goes in v5:
time: 149 us; the launch traced here: 147 us
  Pallas kernels  138 us (93%)
  local copies, waits for them, and re-layouts  7.78 us (5%)
    pallas_call x1, Pallas kernels, shards(): pl.pallas_call(functools.partial(spread_kernel, chips, tiles), out_shape=...  48.1 us
    pallas_call x1, Pallas kernels, shards(): pl.pallas_call(functools.partial(stencil_kernel, tiles, block), out_shape...  39.9 us
    pallas_call x1, Pallas kernels, shards(): pl.pallas_call(functools.partial(edge_kernel, chips, tiles), out_shape=(j...  25.8 us
    pallas_call x1, Pallas kernels, shards(): pl.pallas_call(functools.partial(join_kernel, groups, 1.0 / (rows * colum...  24.5 us
    unnamed x18, local copies, waits for them, and re-layouts  7.78 us

profile of v5, /device:TPU:0, one launch (start us, length us, event | category | flops | bytes accessed | tf_op | source)
XLA Modules:
  0.0 146.8 jit_solution(6162958753327498125)
XLA Ops:
  0.6 0.0 copy-start
  0.6 3.4 %copy-done = f32[256,16,512]{2,1,0:T(8,128)S(1)} copy-done((f32[256,16,512]{2,1,0:T(8,128)S(1)}, f32[256,16,512]{2,1,0:T(8,128)}, u32[]{:S(2)}) %copy-start) | copy-done | bytes 8388632
  4.0 0.0 copy-start.1
  4.0 0.8 copy-done.1
  4.8 0.0 copy-start.2
  4.8 0.8 copy-done.2
  5.5 0.0 copy-start.3
  5.5 0.8 copy-done.3
  6.3 0.0 copy-start.4
  6.3 0.8 copy-done.4
  7.1 0.0 copy-start.5
  7.1 0.7 copy-done.5
  7.7 0.0 copy-start.6
  7.7 0.7 copy-done.6
  8.4 0.0 slice-start
  8.4 25.8 %edges.1 = (f32[6,256,512]{2,1,0:T(8,128)S(1)}, f32[6,8,512]{2,1,0:T(8,128)S(1)}, f32[264,256]{1,0:T(8,128)S(1)}) custom-call(f32[256,16,512]{2,1,0:T(8,128)S(1)} %copy-done, f32[16,512]{1,0:T(8,128)S(1)} %bitcast.7, f32[16,512]{1,0:T(8,128)S(1)} %bitcast.9, f32[16,512]{1,0:T(8,128)S(1)} %bitcast.11, s32[16,512]{1,0:T(8,128)S(1)} %copy-done.4, ...), custom_call_target="tpu_custom_call" | custom-call | tf_op jit(solution)/shard_map/edges/pallas_call | solution.py:555
  34.2 0.0 slice-start.1
  34.3 39.9 %propagate.1.part_ref = f32[8,72,256]{2,1,0:T(8,128)S(1)} custom-call(f32[256,16,512]{2,1,0:T(8,128)} %basis_ref.5, f32[16,512]{1,0:T(8,128)S(1)} %bitcast.8, f32[16,512]{1,0:T(8,128)S(1)} %bitcast.10, f32[16,512]{1,0:T(8,128)S(1)} %bitcast.12, s32[16,512]{1,0:T(8,128)S(1)} %copy-done.4, f32[6,8,512]{2,1,0:T(8,128)S(1)} %get-tuple-element.7.fringe_ref, ...), custom_call_target="tpu_custom_call" | custom-call | flops 41943040000 | bytes 8388608 | tf_op jit(solution)/shard_map/propagate/pallas_call | solution.py:581
  74.1 48.1 %spread.1.sums_ref = f32[4,8,72,256]{3,2,1,0:T(8,128)S(1)} custom-call(f32[8,72,256]{2,1,0:T(8,128)S(1)} %propagate.1.part_ref), custom_call_target="tpu_custom_call" | custom-call | tf_op jit(solution)/shard_map/spread/pallas_call | solution.py:600
  122.2 0.0 slice-done
  122.2 0.0 slice-done.1
  122.2 24.5 %join.1 = (f32[2,256]{1,0:T(2,128)}, f32[16,512]{1,0:T(8,128)}) custom-call(f32[4,8,72,256]{3,2,1,0:T(8,128)S(1)} %spread.1.sums_ref, f32[256,16,512]{2,1,0:T(8,128)S(1)} %bitcast.6), custom_call_target="tpu_custom_call" | custom-call | tf_op jit(solution)/shard_map/join/pallas_call | solution.py:614
  (1 shorter events, 0.0 us)
Async XLA Ops:
  0.6 3.4 %copy-start = (f32[256,16,512]{2,1,0:T(8,128)S(1)}, f32[256,16,512]{2,1,0:T(8,128)}, u32[]{:S(2)}) copy-start(f32[256,16,512]{2,1,0:T(8,128)} %basis_ref.5) | copy-start | bytes 25165828
  4.0 0.8 copy-start.1
  4.8 0.8 copy-start.2
  5.5 0.8 copy-start.3
  6.3 0.8 copy-start.4
  7.1 0.7 copy-start.5
  7.7 0.7 copy-start.6
  8.4 113.8 %slice-start = ((s8[8388608]{0:T(1024)(128)(4,1)}), s8[4194304]{0:T(1024)(128)(4,1)S(1)}, s32[]{:S(2)}) async-start(s8[8388608]{0:T(1024)(128)(4,1)} %bitcast.5), calls=%async_computation | async-start | bytes 8388608
  34.2 88.0 %slice-start.1 = ((s8[8388608]{0:T(1024)(128)(4,1)}), s8[4194304]{0:T(1024)(128)(4,1)S(1)}, s32[]{:S(2)}) async-start(s8[8388608]{0:T(1024)(128)(4,1)} %bitcast.5), calls=%async_computation.1 | async-start | bytes 8388608
